TPU v7x, 32 devices: a whole 2x2x4 slice. The times are simulated.
32 devices in a mesh: pipe: 2 (over y), lat: 4 (over x, core), lon: 4 (over z).
Axes of the slice: x: 2, y: 2, z: 4, core: 2. Of those that a mesh axis runs over, the one named last changes fastest.
Arguments:
- field: bfloat16 [192, 64, 1024], P(None, 'lat', 'lon'), may hold values from -6 to 6
- conv_weight: bfloat16 [192, 1728], replicated, may hold values from -0.15625 to 0.15625
- conv_bias: float32 [192], replicated, may hold values from -3 to 3
- expand_weight: bfloat16 [768, 192], replicated, may hold values from -0.4375 to 0.4375
- expand_bias: float32 [768], replicated, may hold values from -3 to 3
- project_weight: bfloat16 [192, 768], replicated, may hold values from -0.21875 to 0.21875
- project_bias: float32 [192], replicated, may hold values from -3 to 3
- out_cotangent: bfloat16 [192, 32, 512], P(None, 'lat', 'lon'), may hold values from -6 to 6
- dropout_key: int32 [2], replicated, may hold values from 0 to 1073741823
Outputs:
- section_fields: bfloat16 [2, 192, 32, 512], P('pipe', None, 'lat', 'lon')
- conv_grad: float32 [192, 1728], replicated
- conv_bias_grad: float32 [192], replicated
- expand_grad: float32 [768, 192], replicated
- expand_bias_grad: float32 [768], replicated
- project_grad: float32 [192, 768], replicated
- project_bias_grad: float32 [192], replicated
All inputs are finite; a program needn't handle non-finite values.
Results may differ from a plain program's by a relative error of at most 0.0056.
Values may be sent and summed in bfloat16 or wider, within the bound.
A program may use at most 64 MiB of HBM per device.

v0:
```python
import jax
import jax.numpy as jnp
from jax import lax
from jax.sharding import PartitionSpec as P

MIXER_ONE = -2048144789
MIXER_TWO = -1028477387
GOLDEN_STEP = -1640531535
KEEP_LEVEL = 819
KEEP_SCALE = 1024.0 / 819.0


def passed_along(value, axis, steps):
    count = lax.axis_size(axis)
    pairs = [(source, (source + steps) % count) for source in range(count)]
    return lax.ppermute(value, axis, pairs)


def shifted_2(block, axis, distance):
    devices = range(lax.axis_size(axis))
    route = [(i - distance, i) for i in devices if i - distance in devices]
    return lax.ppermute(block, axis, route)


def shifted(number, places):
    return lax.shift_right_logical(number, jnp.full_like(number, places))


def scramble(number):
    number = number ^ shifted(number, 16)
    number = number * jnp.int32(MIXER_ONE)
    number = number ^ shifted(number, 13)
    number = number * jnp.int32(MIXER_TWO)
    return number ^ shifted(number, 16)


def keep_mask(cell_index, dropout_key):
    salt = scramble(dropout_key[0] + scramble(dropout_key[1]))
    hashed = scramble(cell_index * jnp.int32(GOLDEN_STEP) + salt)
    bucket = jnp.bitwise_and(shifted(hashed, 8), jnp.int32(1023))
    return jnp.where(bucket < KEEP_LEVEL, jnp.float32(KEEP_SCALE), jnp.float32(0.0))


def gelu_slope(point, incoming):
    return jax.vjp(jax.nn.gelu, point)[1](incoming)[0]


def outer_sum(left, right):
    return lax.dot_general(
        left, right, (((1,), (1,)), ((), ())), preferred_element_type=jnp.float32
    )


def contract_first(weight, right):
    return lax.dot_general(
        weight, right, (((0,), (0,)), ((), ())), preferred_element_type=jnp.float32
    )


def parity_planes(padded, out_rows, out_cols):
    channels = padded.shape[0]
    even_sized = jnp.pad(padded, ((0, 0), (0, 1), (0, 1)))
    split = even_sized.reshape(channels, out_rows + 1, 2, out_cols + 1, 2)
    return jnp.transpose(split, (2, 4, 0, 1, 3))


def tap_slice(planes, tap_row, tap_col, out_rows, out_cols):
    plane = planes[tap_row % 2, tap_col % 2]
    channels = plane.shape[0]
    row_from = tap_row // 2
    col_from = tap_col // 2
    piece = lax.slice(
        plane, (0, row_from, col_from), (channels, row_from + out_rows, col_from + out_cols)
    )
    return piece.reshape(channels, out_rows * out_cols)


def convolve(conv_weight, planes, out_rows, out_cols):
    channels = planes.shape[2]
    total = None
    for tap_row in range(3):
        for tap_col in range(3):
            tap = 3 * tap_row + tap_col
            term = jnp.dot(
                conv_weight[:, tap * channels : (tap + 1) * channels],
                tap_slice(planes, tap_row, tap_col, out_rows, out_cols),
                preferred_element_type=jnp.float32,
            )
            total = term if total is None else total + term
    return total


def kernel_gradient(d_half, planes, out_rows, out_cols):
    blocks = []
    for tap_row in range(3):
        for tap_col in range(3):
            blocks.append(
                outer_sum(d_half, tap_slice(planes, tap_row, tap_col, out_rows, out_cols))
            )
    return jnp.concatenate(blocks, axis=1)


def hand_over(payload):
    return passed_along(payload, "pipe", 1)


def per_device(
    field,
    conv_weight,
    conv_bias,
    expand_weight,
    expand_bias,
    project_weight,
    project_bias,
    out_cotangent,
    dropout_key,
):
    channels, row_count, col_count = field.shape
    hidden_count = expand_weight.shape[0]
    half_rows = row_count // 2
    half_cols = col_count // 2
    lat_count = lax.axis_size("lat")
    lon_count = lax.axis_size("lon")
    scale = float(half_rows * lat_count * half_cols * lon_count) ** (-0.5)
    pipe_index = lax.axis_index("pipe")
    is_encoder = pipe_index == 0
    from_above = shifted_2(field[:, row_count - 1 :, :], "lat", 1)
    mirrored = passed_along(field[:, :1, :], "lon", lon_count // 2)
    top_row = jnp.where(lax.axis_index("lat") == 0, mirrored, from_above)
    extended = jnp.concatenate([top_row, field], axis=1)
    west_edge = passed_along(extended[:, :, col_count - 1 :], "lon", 1)
    padded = jnp.concatenate([west_edge, extended], axis=2)
    row_start = 0
    cell_count = half_rows * half_cols
    planes = parity_planes(padded, half_rows, half_cols)
    row_ids = lax.axis_index("lat") * half_rows + row_start + jnp.arange(half_rows, dtype=jnp.int32)
    col_ids = lax.axis_index("lon") * half_cols + jnp.arange(half_cols, dtype=jnp.int32)
    cell_ids = (row_ids[:, None] * (half_cols * lon_count) + col_ids[None, :]).reshape(-1)
    keep = keep_mask(cell_ids, dropout_key)[None, :]

    def encode():
        pre = convolve(conv_weight, planes, half_rows, half_cols) + conv_bias[:, None]
        encoded = (jax.nn.gelu(pre) * keep).astype(jnp.bfloat16)
        return (encoded, pre)

    def encode_empty():
        return (
            jnp.zeros((channels, cell_count), jnp.bfloat16),
            jnp.zeros((channels, cell_count), jnp.float32),
        )

    def process(received):
        inner = (
            jnp.dot(expand_weight, received, preferred_element_type=jnp.float32)
            + expand_bias[:, None]
        )
        activated = jax.nn.gelu(inner).astype(jnp.bfloat16)
        processed = (
            received.astype(jnp.float32)
            + jnp.dot(project_weight, activated, preferred_element_type=jnp.float32)
            + project_bias[:, None]
        ).astype(jnp.bfloat16)
        scaled = out_cotangent.reshape(channels, cell_count).astype(jnp.float32) * scale
        cot_half = scaled.astype(jnp.bfloat16)
        project_grad = outer_sum(cot_half, activated)
        d_inner = gelu_slope(inner, contract_first(project_weight, cot_half))
        d_inner_half = d_inner.astype(jnp.bfloat16)
        expand_grad = outer_sum(d_inner_half, received)
        d_encoded = (scaled + contract_first(expand_weight, d_inner_half)).astype(jnp.bfloat16)
        flat = jnp.concatenate(
            [
                expand_grad.reshape(-1),
                jnp.sum(d_inner, axis=1),
                project_grad.reshape(-1),
                jnp.sum(scaled, axis=1),
            ]
        )
        return (processed, d_encoded, flat)

    enc_len = conv_weight.size + channels
    proc_len = 2 * expand_weight.size + hidden_count + channels

    def process_empty():
        return (
            jnp.zeros((channels, cell_count), jnp.bfloat16),
            jnp.zeros((channels, cell_count), jnp.bfloat16),
            jnp.zeros((proc_len,), jnp.float32),
        )

    def backward(pre_now, d_encoded_now):
        d_pre = gelu_slope(pre_now, d_encoded_now.astype(jnp.float32) * keep)
        conv_grad = kernel_gradient(d_pre.astype(jnp.bfloat16), planes, half_rows, half_cols)
        return jnp.concatenate([conv_grad.reshape(-1), jnp.sum(d_pre, axis=1)])

    def backward_empty():
        return jnp.zeros((enc_len,), jnp.float32)

    encoded, pre_saved = lax.cond(is_encoder, encode, encode_empty)
    received = hand_over(encoded)
    processed, d_encoded, flat_proc = lax.cond(is_encoder, process_empty, lambda: process(received))
    returned = hand_over(d_encoded)
    flat_enc = lax.cond(is_encoder, lambda: backward(pre_saved, returned), backward_empty)
    section_fields = jnp.where(is_encoder, encoded, processed).reshape(
        1, channels, half_rows, half_cols
    )
    combined = jnp.concatenate([flat_enc, flat_proc])
    total = lax.psum(combined, ("pipe", "lat", "lon"))
    enc_total = total[:enc_len]
    proc_total = total[enc_len:]
    weight_count = conv_weight.size
    conv_grad = enc_total[:weight_count].reshape(conv_weight.shape)
    conv_bias_grad = enc_total[weight_count:]
    expand_count = expand_weight.size
    expand_grad = proc_total[:expand_count].reshape(expand_weight.shape)
    expand_bias_grad = proc_total[expand_count : expand_count + hidden_count]
    project_start = expand_count + hidden_count
    project_grad = proc_total[project_start : project_start + expand_count].reshape(
        project_weight.shape
    )
    project_bias_grad = proc_total[project_start + expand_count :]
    return (
        section_fields,
        conv_grad,
        conv_bias_grad,
        expand_grad,
        expand_bias_grad,
        project_grad,
        project_bias_grad,
    )


def solution(mesh):
    placed = (P(None, "lat", "lon"), P(), P(), P(), P(), P(), P(), P(None, "lat", "lon"), P())
    return jax.shard_map(
        per_device,
        mesh=mesh,
        in_specs=placed,
        out_specs=(P("pipe", None, "lat", "lon"), P(), P(), P(), P(), P(), P()),
        check_vma=False,
    )
```

profile of v0, /device:TPU:0, one launch (start us, length us, event | category | flops | bytes accessed | tf_op | source)
XLA Modules:
  0.0 278.3 jit_solution(14114148621795843833)
XLA Ops:
  7.2 1.7 fusion.114
  8.9 4.1 %collective-permute-start = (bf16[192,1,256]{2,0,1:T(8,128)(2,1)S(1)}, bf16[192,1,256]{2,0,1:T(8,128)(2,1)S(1)}, u32[]{:S(2)}, u32[]{:S(2)}) collective-permute-start(bf16[192,1,256]{2,0,1:T(8,128)(2,1)S(1)} %copy.47), channel_id=1, source_target_pairs={{0,2},{1,3},{2,0},{3,1},{4,6},{5,7},{6,4},{7,5},{8,10},{9,11},{10,... | collective-permute-start | bytes 294920 | tf_op jit(solution)/shard_map/ppermute | solution.py:16
  13.0 1.5 collective-permute-start.1
  17.9 3.6 %copy.37 = bf16[192,16,256]{0,1,2:T(8,128)(2,1)S(1)} copy(bf16[192,16,256]{2,1,0:T(8,128)(2,1)} %param.15) | data formatting | bytes 3145728 | tf_op args[0]
  21.8 1.6 collective-permute-start.2
  23.4 3.9 %collective-permute-done.2 = bf16[192,17,1]{0,1,2:T(8,128)(2,1)S(1)} collective-permute-done((bf16[192,17,1]{0,1,2:T(8,128)(2,1)S(1)}, bf16[192,17,1]{0,1,2:T(8,128)(2,1)S(1)}, u32[]{:S(2)}, u32[]{:S(2)}) %collective-permute-start.2) | collective-permute-done | bytes 6560 | tf_op jit(solution)/shard_map/ppermute | solution.py:16
  27.3 2.7 fusion.97
  30.0 6.4 %reshape.189 = bf16[192,9,2,129,2]{0,2,1,4,3:T(2,128)(2,1)} reshape(bf16[192,18,258]{0,1,2:T(8,128)(2,1)} %fusion.97) | data formatting | bytes 3566592 | tf_op jit(solution)/shard_map/reshape | solution.py:63
  36.4 3.5 %copy.150 = bf16[192,9,2,129,2]{0,4,3,2,1:T(2,128)(2,1)S(1)} copy(bf16[192,9,2,129,2]{0,2,1,4,3:T(2,128)(2,1)} %reshape.189) | data formatting | bytes 3566592 | tf_op jit(solution)/shard_map/reshape | solution.py:63
  40.0 19.9 %conditional.3 = ((bf16[192,1024]{1,0:T(8,128)(2,1)}, f32[192,1024]{1,0:T(8,128)S(1)})) conditional(s32[]{:T(128)} %convert_element_type.39, () %tuple.30, (bf16[192,1728]{1,0:T(8,128)(2,1)}, bf16[2,2,192,9,129]{2,1,4,0,3:T(2,128)(2,1)S(1)}, f32[192]{0:T(256)S(1)}, f32[1,1024]{1,0:T(1,128)S(1)}) %tuple.92), branch_computations={%region_0.1_spmd, %region_1.2_spmd} | conditional | flops 683212800 | bytes 35056676 | solution.py:198
  40.0 11.7 %copy.39 = bf16[2,2,192,9,129]{4,3,2,1,0:T(8,128)(2,1)} copy(bf16[2,2,192,9,129]{2,1,4,0,3:T(2,128)(2,1)S(1)} %get-tuple-element.104) | data formatting | bytes 3566592 | tf_op jit(solution)/shard_map
  51.7 3.2 %slice_bitcast_fusion = (bf16[192,9,129]{2,1,0:T(8,128)(2,1)S(1)}, bf16[192,9,129]{2,1,0:T(8,128)(2,1)S(1)}, bf16[192,9,129]{2,1,0:T(8,128)(2,1)S(1)}, bf16[192,9,129]{2,1,0:T(8,128)(2,1)S(1)}) fusion(bf16[2,2,192,9,129]{4,3,2,1,0:T(8,128)(2,1)} %copy.39), kind=kLoop, calls=%fused_computation | loop fusion | bytes 3566592 | tf_op jit(solution)/shard_map/cond/branch_1_fun/squeeze | solution.py:68
  59.9 12.1 %collective-permute-done.3 = bf16[192,1024]{1,0:T(8,128)(2,1)S(1)} collective-permute-done((bf16[192,1024]{1,0:T(8,128)(2,1)}, bf16[192,1024]{1,0:T(8,128)(2,1)S(1)}, u32[]{:S(2)}, u32[]{:S(2)}) %collective-permute-start.3) | collective-permute-done | bytes 393248 | tf_op jit(solution)/shard_map/ppermute | solution.py:16
  72.4 19.1 %collective-permute-start.4 = (bf16[192,1024]{1,0:T(8,128)(2,1)S(1)}, bf16[192,1024]{1,0:T(8,128)(2,1)}, u32[]{:S(2)}, u32[]{:S(2)}) collective-permute-start(bf16[192,1024]{1,0:T(8,128)(2,1)S(1)} %get-tuple-element.59), channel_id=1, source_target_pairs={{0,16},{16,0},{1,17},{17,1},{2,18},{18,2},{3,19},{19,3},{4,20},{20... | collective-permute-start | bytes 1179656 | tf_op jit(solution)/shard_map/ppermute | solution.py:16
  91.5 9.5 %collective-permute-done.4 = bf16[192,1024]{1,0:T(8,128)(2,1)} collective-permute-done((bf16[192,1024]{1,0:T(8,128)(2,1)S(1)}, bf16[192,1024]{1,0:T(8,128)(2,1)}, u32[]{:S(2)}, u32[]{:S(2)}) %collective-permute-start.4) | collective-permute-done | bytes 393248 | tf_op jit(solution)/shard_map/ppermute | solution.py:16
  101.1 25.0 %conditional.5 = (f32[331968]{0:T(1024)S(1)}) conditional(s32[]{:T(128)} %convert_element_type.39, () %tuple.34, (bf16[192,1024]{1,0:T(8,128)(2,1)}, f32[1,1024]{1,0:T(1,128)S(1)}, f32[192,1024]{1,0:T(8,128)}, bf16[2,2,192,9,129]{2,1,4,0,3:T(2,128)(2,1)S(1)}) %tuple.88), branch_computations={%region_6.7_spmd, %region_7.9_spmd} | conditional | flops 684331008 | bytes 36876584 | solution.py:202
  101.1 11.7 %copy.41 = bf16[2,2,192,9,129]{4,3,2,1,0:T(8,128)(2,1)} copy(bf16[2,2,192,9,129]{2,1,4,0,3:T(2,128)(2,1)S(1)} %get-tuple-element.116) | data formatting | bytes 3566592 | tf_op jit(solution)/shard_map
  112.7 3.2 %slice_bitcast_fusion.4 = (bf16[192,9,129]{2,1,0:T(8,128)(2,1)S(1)}, bf16[192,9,129]{2,1,0:T(8,128)(2,1)S(1)}, bf16[192,9,129]{2,1,0:T(8,128)(2,1)S(1)}, bf16[192,9,129]{2,1,0:T(8,128)(2,1)S(1)}) fusion(bf16[2,2,192,9,129]{4,3,2,1,0:T(8,128)(2,1)} %copy.41), kind=kLoop, calls=%fused_computation.80 | loop fusion | bytes 3566592 | tf_op jit(solution)/shard_map/cond/branch_1_fun/squeeze | solution.py:68
  117.1 1.6 fusion.103
  126.0 3.2 %pad_maximum_fusion.2 = f32[627840]{0:T(1024)} fusion(f32[295872]{0:T(1024)} %copy-done.4, f32[331968]{0:T(1024)S(1)} %get-tuple-element.183), kind=kLoop, calls=%fused_computation.131 | loop fusion | flops 627840 | bytes 5022720 | tf_op jit(solution)/shard_map/concatenate | solution.py:206
  131.2 129.0 %all-reduce.3.cloned.1.call-done = f32[627840]{0:T(1024)} async-done(((f32[627840]{0:T(1024)}), f32[627840]{0:T(1024)}) %all-reduce.3.cloned.1.call-update) | async-done | bytes 2511376 | tf_op jit(solution)/shard_map/psum | solution.py:207
  261.5 1.5 reshape.186
  263.0 2.6 fusion.113
  268.1 2.0 reshape.188
  (79 shorter events, 22.5 us)
Async XLA Ops:
  7.2 253.0 %all-reduce.3.cloned.1.call-start = ((), (), s32[]{:S(2)}) async-start(), calls=%async_computation | async-start | bytes 5029888 | tf_op jit(solution)/shard_map/psum | solution.py:207
  8.9 12.6 %collective-permute-start = (bf16[192,1,256]{2,0,1:T(8,128)(2,1)S(1)}, bf16[192,1,256]{2,0,1:T(8,128)(2,1)S(1)}, u32[]{:S(2)}, u32[]{:S(2)}) collective-permute-start(bf16[192,1,256]{2,0,1:T(8,128)(2,1)S(1)} %copy.47), channel_id=1, source_target_pairs={{0,2},{1,3},{2,0},{3,1},{4,6},{5,7},{6,4},{7,5},{8,10},{9,11},{10,... | collective-permute-start | bytes 294920 | tf_op jit(solution)/shard_map/ppermute | solution.py:16
  13.0 8.5 %collective-permute-start.1 = (bf16[192,1,256]{2,0,1:T(8,128)(2,1)S(1)}, bf16[192,1,256]{2,0,1:T(8,128)(2,1)S(1)}, u32[]{:S(2)}, u32[]{:S(2)}) collective-permute-start(bf16[192,1,256]{2,0,1:T(8,128)(2,1)S(1)} %copy.48), channel_id=1, source_target_pairs={{0,4},{4,8},{8,12},{1,5},{5,9},{9,13},{2,6},{6,10},{10,14},{3,7},{... | collective-permute-start | bytes 294920 | tf_op jit(solution)/shard_map/ppermute | solution.py:22
  21.8 5.5 %collective-permute-start.2 = (bf16[192,17,1]{0,1,2:T(8,128)(2,1)S(1)}, bf16[192,17,1]{0,1,2:T(8,128)(2,1)S(1)}, u32[]{:S(2)}, u32[]{:S(2)}) collective-permute-start(bf16[192,17,1]{0,1,2:T(8,128)(2,1)S(1)} %pad_maximum_fusion.3), channel_id=1, source_target_pairs={{0,1},{1,2},{2,3},{3,0},{4,5},{5,6},{6,7},{7,4},{8,9},{9,10},{10,1... | collective-permute-start | bytes 19592 | tf_op jit(solution)/shard_map/ppermute | solution.py:16
  36.4 3.5 %copy-start.19 = (f32[192]{0:T(256)S(1)}, f32[192]{0:T(256)}, u32[]{:S(2)}) copy-start(f32[192]{0:T(256)} %param.17) | copy-start | bytes 2308
  40.0 32.0 %copy-start.14 = (bf16[768,192]{0,1:T(8,128)(2,1)S(1)}, bf16[768,192]{0,1:T(8,128)(2,1)}, u32[]{:S(2)}) copy-start(bf16[768,192]{0,1:T(8,128)(2,1)} %param.18) | copy-start | bytes 884740
  40.0 32.0 %copy-start.17 = (f32[192]{0:T(256)S(1)}, f32[192]{0:T(256)}, u32[]{:S(2)}) copy-start(f32[192]{0:T(256)} %param.21) | copy-start | bytes 2308
  40.0 32.0 %copy-start.18 = (f32[768]{0:T(1024)S(1)}, f32[768]{0:T(1024)}, u32[]{:S(2)}) copy-start(f32[768]{0:T(1024)} %param.19) | copy-start | bytes 9220
  55.0 1.1 copy-start.12
  59.9 12.1 %copy-start.5 = (f32[192,1024]{1,0:T(8,128)}, f32[192,1024]{1,0:T(8,128)S(1)}, u32[]{:S(2)}) copy-start(f32[192,1024]{1,0:T(8,128)S(1)} %get-tuple-element.60) | copy-start | bytes 2359300
  59.9 12.1 %collective-permute-start.3 = (bf16[192,1024]{1,0:T(8,128)(2,1)}, bf16[192,1024]{1,0:T(8,128)(2,1)S(1)}, u32[]{:S(2)}, u32[]{:S(2)}) collective-permute-start(bf16[192,1024]{1,0:T(8,128)(2,1)} %get-tuple-element.57), channel_id=1, source_target_pairs={{0,16},{16,0},{1,17},{17,1},{2,18},{18,2},{3,19},{19,3},{4,20},{20... | collective-permute-start | bytes 1179656 | tf_op jit(solution)/shard_map/ppermute | solution.py:16
  72.4 28.6 %copy-start.4 = (f32[295872]{0:T(1024)}, f32[295872]{0:T(1024)S(1)}, u32[]{:S(2)}) copy-start(f32[295872]{0:T(1024)S(1)} %get-tuple-element.61) | copy-start | bytes 3550468
  72.4 28.6 %copy-start.7 = (bf16[192,1024]{1,0:T(8,128)(2,1)}, bf16[192,1024]{1,0:T(8,128)(2,1)S(1)}, u32[]{:S(2)}) copy-start(bf16[192,1024]{1,0:T(8,128)(2,1)S(1)} %get-tuple-element.58) | copy-start | bytes 1179652
  72.4 28.6 %collective-permute-start.4 = (bf16[192,1024]{1,0:T(8,128)(2,1)S(1)}, bf16[192,1024]{1,0:T(8,128)(2,1)}, u32[]{:S(2)}, u32[]{:S(2)}) collective-permute-start(bf16[192,1024]{1,0:T(8,128)(2,1)S(1)} %get-tuple-element.59), channel_id=1, source_target_pairs={{0,16},{16,0},{1,17},{17,1},{2,18},{18,2},{3,19},{19,3},{4,20},{20... | collective-permute-start | bytes 1179656 | tf_op jit(solution)/shard_map/ppermute | solution.py:16
  116.0 1.1 copy-start.6
  129.2 1.0 copy-start.8
  129.2 1.1 copy-start.9
  260.2 1.3 slice-start
  265.7 4.5 %copy-start.3 = (f32[627840]{0:T(1024)S(1)}, f32[627840]{0:T(1024)}, u32[]{:S(2)}) copy-start(f32[627840]{0:T(1024)} %all-reduce.3.cloned.1.call-done) | copy-start | bytes 7534084
Sparse Core Ops, SparseCore 0:
  129.4 130.8 all-reduce.2
where the time goes:
time: 279 us; the launch traced here: 278 us
  waiting for transfers between devices  155 us (56%)
  local copies, waits for them, and re-layouts  64.8 us (23%)
  starting transfers between devices  26.4 us (9%)
  between operations  16.2 us (6%)
  matrix products  8.09 us (3%)
  other arithmetic  7.87 us (3%)
    psum x1, waiting for transfers between devices, per_device(): total = lax.psum(combined, ('pipe', 'lat', 'lon'))  129 us
    ppermute x4, waiting for transfers between devices, passed_along(): return lax.ppermute(value, axis, pairs)  25.5 us
    ppermute x4, starting transfers between devices, passed_along(): return lax.ppermute(value, axis, pairs)  24.9 us
    another operation x5, local copies, waits for them, and re-layouts  23.6 us
    reshape x2, local copies, waits for them, and re-layouts, parity_planes(): split = even_sized.reshape(channels, out_rows + 1, 2, out_cols + 1, 2)  9.93 us
    unnamed x25, local copies, waits for them, and re-layouts  6.66 us
    squeeze x2, local copies, waits for them, and re-layouts, tap_slice(): plane = planes[tap_row % 2, tap_col % 2]  6.47 us
  transfers between devices with their start and end apart: 6, of which 4 were waited for; matrix products, arithmetic and copies ran while one was open for 2% of the time, Pallas kernels for 0%

commit v1 on v0

v1 whole, which is shorter than its diff:
```python
import functools

import jax
import jax.numpy as jnp
from jax import lax
from jax.experimental import pallas as pl
from jax.experimental.pallas import tpu as pltpu
from jax.sharding import PartitionSpec as P

MIXER_ONE = -2048144789
MIXER_TWO = -1028477387
GOLDEN_STEP = -1640531535
KEEP_LEVEL = 819
KEEP_SCALE = 1024.0 / 819.0
ROOT = 0.7978845608028654
CUBIC = 0.044715
MESH = pl.DeviceIdType.MESH
BF = jnp.bfloat16
F32 = jnp.float32


def passed_along(value, axis, steps):
    count = lax.axis_size(axis)
    pairs = [(source, (source + steps) % count) for source in range(count)]
    return lax.ppermute(value, axis, pairs)


def shifted_2(block, axis, distance):
    devices = range(lax.axis_size(axis))
    route = [(i - distance, i) for i in devices if i - distance in devices]
    return lax.ppermute(block, axis, route)


def shifted(number, places):
    return lax.shift_right_logical(number, jnp.full_like(number, places))


def scramble(number):
    number = number ^ shifted(number, 16)
    number = number * jnp.int32(MIXER_ONE)
    number = number ^ shifted(number, 13)
    number = number * jnp.int32(MIXER_TWO)
    return number ^ shifted(number, 16)


def gelu_both(x):
    square = x * x
    t = jnp.tanh(ROOT * (x + CUBIC * (square * x)))
    cdf = 0.5 * (1.0 + t)
    slope = cdf + (0.5 * ROOT) * x * (1.0 - t * t) * (1.0 + (3.0 * CUBIC) * square)
    return x * cdf, slope


def gelu_only(x):
    t = jnp.tanh(ROOT * (x + CUBIC * (x * x * x)))
    return x * (0.5 * (1.0 + t))


def dot(left, right, dims):
    return lax.dot_general(left, right, (dims, ((), ())), preferred_element_type=F32)


NN = ((1,), (0,))
NT = ((1,), (1,))
TN = ((0,), (0,))


def compute_kernel(
    rows,
    cols,
    total_rows,
    scale,
    salt_ref,
    xt,
    top,
    west,
    cw,
    cb,
    ew,
    eb,
    pw,
    pb,
    cot,
    field_out,
    payload,
    patches,
    enc_s,
    act_s,
    cot_s,
    di_s,
    dp_s,
):
    channels, taps = cw.shape
    hidden = ew.shape[0]
    cells = rows * cols
    pad_taps = patches.shape[0]
    is_encoder = lax.axis_index("pipe") == 0
    lon_cols = cols * lax.axis_size("lon")
    row_base = lax.axis_index("lat") * rows
    col_base = lax.axis_index("lon") * cols

    source = lax.broadcasted_iota(jnp.int32, (2 * cols, 3 * cols), 0)
    target = lax.broadcasted_iota(jnp.int32, (2 * cols, 3 * cols), 1)
    tap = target // cols
    wanted = 2 * (target - tap * cols) + tap - 1
    select = jnp.where(source == wanted, 1.0, 0.0).astype(BF)
    edge_row = lax.broadcasted_iota(jnp.int32, (128, cols), 0)
    edge_col = lax.broadcasted_iota(jnp.int32, (128, cols), 1)
    west_edge = west[...]
    for q in range(2 * rows + 1):
        line = top[...] if q == 0 else xt[q - 1]
        split = dot(line, select, NN)
        pick = jnp.where((edge_row == q) & (edge_col == 0), 1.0, 0.0).astype(BF)
        first = (split[:, :cols] + dot(west_edge, pick, NN)).astype(BF)
        parts = [first, split[:, cols : 2 * cols].astype(BF), split[:, 2 * cols :].astype(BF)]
        places = [(1, q // 2)] if q % 2 else [(a, q // 2 - a // 2) for a in (0, 2)]
        for a, r in places:
            if 0 <= r < rows:
                for b in range(3):
                    start = (3 * a + b) * channels
                    patches[start : start + channels, r * cols : (r + 1) * cols] = parts[b]
    patches[taps:, :] = jnp.zeros((pad_taps - taps, cells), BF)

    lanes = lax.broadcasted_iota(jnp.int32, (channels, 128), 1)
    salt = salt_ref[0]
    step = 2 * cols
    sums = [0.0, 0.0, 0.0]
    for j in range(cells // step):
        here = slice(j * step, (j + 1) * step)
        lane = lax.broadcasted_iota(jnp.int32, (1, step), 1)
        local_row = lane // cols
        cell = (row_base + 2 * j + local_row) * lon_cols + col_base + lane - local_row * cols
        hashed = scramble(cell * jnp.int32(GOLDEN_STEP) + salt)
        bucket = jnp.bitwise_and(shifted(hashed, 8), jnp.int32(1023))
        keep = jnp.where(bucket < KEEP_LEVEL, F32(KEEP_SCALE), F32(0.0))
        pre = dot(cw[...], patches[:taps, here], NN) + cb[...]
        value, pre_slope = gelu_both(pre)
        encoded = (value * keep).astype(BF)
        inner = dot(ew[...], encoded, NN) + eb[...]
        activated, slope = gelu_both(inner)
        activated = activated.astype(BF)
        scaled = jnp.concatenate([cot[2 * j], cot[2 * j + 1]], axis=1).astype(F32) * scale
        cot_half = scaled.astype(BF)
        d_inner = dot(pw[...], cot_half, TN) * slope
        d_half = d_inner.astype(BF)

        def encoder_part(sums=sums):
            field_out[2 * j] = encoded[:, :cols]
            field_out[2 * j + 1] = encoded[:, cols:]
            d_encoded = (scaled + dot(ew[...], d_half, TN)).astype(BF)
            d_pre = d_encoded.astype(F32) * keep * pre_slope
            dp_s[:, here] = d_pre.astype(BF)
            act_s[0:channels, j * 128 : j * 128 + 128] = jnp.sum(d_pre, axis=1, keepdims=True) + jnp.zeros(
                (channels, 128), F32
            )

        def processor_part():
            processed = (encoded.astype(F32) + dot(pw[...], activated, NN) + pb[...]).astype(BF)
            field_out[2 * j] = processed[:, :cols]
            field_out[2 * j + 1] = processed[:, cols:]
            enc_s[:, here] = encoded
            cot_s[:, here] = cot_half
            di_s[:hidden, here] = activated
            di_s[hidden:, here] = d_half
            bias = jnp.where(lanes == 0, jnp.sum(scaled, axis=1, keepdims=True), 0.0)
            total = jnp.sum(d_inner, axis=1, keepdims=True)
            for k in range(hidden // channels):
                bias = jnp.where(lanes == k + 1, total[k * channels : (k + 1) * channels], bias)
            act_s[0:channels, j * 128 : j * 128 + 128] = bias

        pl.when(is_encoder)(encoder_part)
        pl.when(jnp.logical_not(is_encoder))(processor_part)

    def bias_total():
        total = act_s[:, 0:128]
        for j in range(1, cells // step):
            total = total + act_s[:, j * 128 : j * 128 + 128]
        return total

    blocks = pad_taps // 128

    @pl.when(is_encoder)
    def _():
        for k in range(blocks):
            block = dot(dp_s[...], patches[k * 128 : (k + 1) * 128, :], NT)
            if k == blocks - 1:
                block = jnp.where(lanes == taps - k * 128, bias_total(), block)
            payload[k * channels : (k + 1) * channels, :] = block.astype(BF)

    @pl.when(jnp.logical_not(is_encoder))
    def _():
        per = hidden // 128
        for k in range(per):
            block = dot(cot_s[...], di_s[k * 128 : (k + 1) * 128, :], NT)
            payload[k * channels : (k + 1) * channels, :] = block.astype(BF)
        for k in range(per):
            block = dot(enc_s[...], di_s[hidden + k * 128 : hidden + (k + 1) * 128, :], NT)
            payload[(per + k) * channels : (per + k + 1) * channels, :] = block.astype(BF)
        payload[2 * per * channels : (2 * per + 1) * channels, :] = bias_total().astype(BF)
        rest = (2 * per + 1) * channels
        payload[rest : blocks * channels, :] = jnp.zeros((blocks * channels - rest, 128), BF)

    payload[blocks * channels :, :] = jnp.zeros((total_rows - blocks * channels, 128), BF)


def reduce_kernel(
    n_x, n_z, payload, out, buf1, s1, buf2, s2, buf3, send, recv
):
    pipe = lax.axis_index("pipe")
    lat = lax.axis_index("lat")
    z = lax.axis_index("lon")
    x = lat // 2
    core = lat % 2
    total_rows = payload.shape[0]
    half = total_rows // 2
    part = half // n_x
    own = part // n_z
    twin = (pipe, 2 * x + 1 - core, z)

    def z_peer(d):
        return (pipe, lat, (z + d) % n_z)

    def xp_peer(dx, dp):
        return ((pipe + dp) % 2, 2 * ((x + dx) % n_x) + core, z)

    others = [(dx, dp) for dp in range(2) for dx in range(n_x) if dx or dp]
    peers = [twin] + [z_peer(d) for d in range(1, n_z)] + [xp_peer(*o) for o in others]
    barrier = pltpu.get_barrier_semaphore()
    for peer in peers:
        pl.semaphore_signal(barrier, inc=1, device_id=peer, device_id_type=MESH)
    pl.semaphore_wait(barrier, len(peers))

    count = [0]
    started = []

    def push(src, dst, peer):
        i = count[0]
        count[0] += 1
        copy = pltpu.make_async_remote_copy(
            src_ref=src,
            dst_ref=dst,
            send_sem=send.at[i],
            recv_sem=recv.at[i],
            device_id=peer,
            device_id_type=MESH,
        )
        copy.start()
        started.append(copy)
        return copy

    def at(start, size):
        return pl.ds(pl.multiple_of(start, 16), size)

    push(payload.at[at((1 - core) * half, half)], buf1, twin).wait_recv()
    s1[...] = (payload[at(core * half, half), :].astype(F32) + buf1[...].astype(F32)).astype(BF)

    arrivals = []
    for d in range(1, n_x):
        arrivals.append(push(s1.at[at(((x + d) % n_x) * part, part)], buf2.at[d - 1], xp_peer(d, 0)))
    total = s1[at(x * part, part), :].astype(F32)
    for d in range(1, n_x):
        arrivals[d - 1].wait_recv()
        total = total + buf2[d - 1].astype(F32)
    s2[...] = total.astype(BF)

    arrivals = []
    for d in range(1, n_z):
        arrivals.append(push(s2.at[at(((z + d) % n_z) * own, own)], buf3.at[d - 1], z_peer(d)))
    total = s2[at(z * own, own), :].astype(F32)
    for d in range(1, n_z):
        arrivals[d - 1].wait_recv()
        total = total + buf3[d - 1].astype(F32)
    mine = out.at[pipe, at(core * half + x * part + z * own, own)]
    mine[...] = total.astype(BF)

    arrivals = [push(mine, mine, z_peer(d)) for d in range(1, n_z)]
    for copy in arrivals:
        copy.wait_recv()
    column = out.at[pipe, at(core * half + x * part, part)]
    arrivals = [push(column, column, xp_peer(*o)) for o in others]
    final = [push(column, column, twin)]
    for (dx, dp), copy in zip(others, arrivals):
        copy.wait_recv()
        block = out.at[(pipe + dp) % 2, at(core * half + ((x - dx + n_x) % n_x) * part, part)]
        final.append(push(block, block, twin))
    for copy in final:
        copy.wait_recv()
    for copy in started:
        copy.wait_send()


def per_device(
    field,
    conv_weight,
    conv_bias,
    expand_weight,
    expand_bias,
    project_weight,
    project_bias,
    out_cotangent,
    dropout_key,
):
    channels, row_count, col_count = field.shape
    hidden = expand_weight.shape[0]
    taps = conv_weight.shape[1]
    rows = row_count // 2
    cols = col_count // 2
    cells = rows * cols
    n_lat = lax.axis_size("lat")
    n_lon = lax.axis_size("lon")
    scale = float(cells * n_lat * n_lon) ** (-0.5)

    from_above = shifted_2(field[:, row_count - 1, :], "lat", 1)
    mirrored = passed_along(field[:, 0, :], "lon", n_lon // 2)
    top = jnp.where(lax.axis_index("lat") == 0, mirrored, from_above)
    edge = jnp.concatenate([top[:, col_count - 1 :], field[:, :, col_count - 1]], axis=1)
    west = passed_along(edge, "lon", 1)
    west = jnp.pad(west, ((0, 0), (0, 128 - row_count - 1)))
    salt = scramble(dropout_key[0] + scramble(dropout_key[1])).reshape(1)

    pad_taps = -(-(taps + 1) // 128) * 128
    blocks = pad_taps // 128
    unit = 16 * n_lat * n_lon
    total_rows = -(-(blocks * channels) // unit) * unit
    vmem = pl.BlockSpec(memory_space=pltpu.VMEM)
    smem = pl.BlockSpec(memory_space=pltpu.SMEM)
    field_out, payload = pl.pallas_call(
        functools.partial(compute_kernel, rows, cols, total_rows, scale),
        out_shape=(
            jax.ShapeDtypeStruct((rows, channels, cols), BF),
            jax.ShapeDtypeStruct((total_rows, 128), BF),
        ),
        in_specs=[smem] + [vmem] * 10,
        out_specs=(vmem, vmem),
        scratch_shapes=[
            pltpu.VMEM((pad_taps, cells), BF),
            pltpu.VMEM((channels, cells), BF),
            pltpu.VMEM((channels, cells // (2 * cols) * 128), F32),
            pltpu.VMEM((channels, cells), BF),
            pltpu.VMEM((2 * hidden, cells), BF),
            pltpu.VMEM((channels, cells), BF),
        ],
        compiler_params=pltpu.CompilerParams(vmem_limit_bytes=40 * 1024 * 1024),
        name="segment",
    )(
        salt,
        jnp.transpose(field, (1, 0, 2)),
        top,
        west,
        conv_weight,
        conv_bias[:, None],
        expand_weight,
        expand_bias[:, None],
        project_weight,
        project_bias[:, None],
        jnp.transpose(out_cotangent, (1, 0, 2)),
    )

    n_x = n_lat // 2
    half = total_rows // 2
    part = half // n_x
    own = part // n_lon
    copies = 1 + (n_x - 1) + 2 * (n_lon - 1) + 2 * (2 * n_x - 1) + 1
    gathered = pl.pallas_call(
        functools.partial(reduce_kernel, n_x, n_lon),
        out_shape=jax.ShapeDtypeStruct((2, total_rows, 128), BF),
        in_specs=[vmem],
        out_specs=vmem,
        scratch_shapes=[
            pltpu.VMEM((half, 128), BF),
            pltpu.VMEM((half, 128), BF),
            pltpu.VMEM((n_x - 1, part, 128), BF),
            pltpu.VMEM((part, 128), BF),
            pltpu.VMEM((n_lon - 1, own, 128), BF),
            pltpu.SemaphoreType.DMA((copies,)),
            pltpu.SemaphoreType.DMA((copies,)),
        ],
        compiler_params=pltpu.CompilerParams(
            collective_id=0, has_side_effects=True, vmem_limit_bytes=40 * 1024 * 1024
        ),
        name="gradient_sum",
    )(payload)

    used = gathered[:, : blocks * channels].reshape(2, blocks, channels, 128)
    wide = used[0].transpose(1, 0, 2).reshape(channels, pad_taps).astype(F32)
    conv_grad = wide[:, :taps]
    conv_bias_grad = wide[:, taps]
    per = hidden // 128
    project_grad = used[1, :per].transpose(1, 0, 2).reshape(channels, hidden).astype(F32)
    expand_grad = used[1, per : 2 * per].transpose(0, 2, 1).reshape(hidden, channels).astype(F32)
    biases = used[1, 2 * per].astype(F32)
    project_bias_grad = biases[:, 0]
    expand_bias_grad = biases[:, 1 : 1 + hidden // channels].T.reshape(hidden)
    section_fields = jnp.transpose(field_out, (1, 0, 2))[None]
    return (
        section_fields,
        conv_grad,
        conv_bias_grad,
        expand_grad,
        expand_bias_grad,
        project_grad,
        project_bias_grad,
    )


def solution(mesh):
    placed = (P(None, "lat", "lon"), P(), P(), P(), P(), P(), P(), P(None, "lat", "lon"), P())
    return jax.shard_map(
        per_device,
        mesh=mesh,
        in_specs=placed,
        out_specs=(P("pipe", None, "lat", "lon"), P(), P(), P(), P(), P(), P()),
        check_vma=False,
    )
```

time: 279 us -> 70.4 us (0.25)
  waiting for transfers between devices: 155 us -> 4.72 us
  local copies, waits for them, and re-layouts: 64.8 us -> 13.7 us
  Pallas kernels: 0 us -> 39.6 us
  starting transfers between devices: 26.4 us -> 7.95 us
  between operations: 16.2 us -> 2.82 us
  matrix products: 8.09 us -> 0 us
  other arithmetic: 7.87 us -> 1.37 us
    psum x1 -> x0, waiting for transfers between devices: 129 us -> none  [per_device(): total = lax.psum(combined, ('pipe', 'lat', 'lon'))]
    pallas_call x0 -> x2, Pallas kernels: none -> 39.6 us  [the longest x1 30.2 us: per_device(): pl.pallas_call(functools.partial(reduce_kernel, n_x, n_lon), out_shape=ja...]
    another operation x5 -> x0, local copies, waits for them, and re-layouts: 23.6 us -> none
    ppermute x4 -> x2, waiting for transfers between devices: 25.5 us -> 4.72 us  [passed_along(): return lax.ppermute(value, axis, pairs)]
    ppermute x4 -> x2, starting transfers between devices: 24.9 us -> 4.95 us  [passed_along(): return lax.ppermute(value, axis, pairs)]
    reshape x6 -> x1, local copies, waits for them, and re-layouts: 15.5 us -> 0.67 us  [per_device(): expand_bias_grad = biases[:, 1:1 + hidden // channels].T.reshape(hidden)]
    dot_general x18 -> x0, matrix products: 8.09 us -> none  [the longest x9 4.63 us: outer_sum(): lax.dot_general(left, right, (((1,), (1,)), ((), ())), preferred_element_...]
    slice x13 -> x9, local copies, waits for them, and re-layouts: 10.3 us -> 2.62 us  [the longest x1 0.92 us: per_device(): conv_bias_grad = wide[:, taps]]
  transfers between devices with their start and end apart: 6 -> 3, of which waited for: 4 -> 2; matrix products, arithmetic and copies ran while one was open for 2% -> 5% of each run, Pallas kernels for 0% -> 0%
where the time goes in v1:
time: 70.4 us; the launch traced here: 70.2 us
  Pallas kernels  39.6 us (56%)
  local copies, waits for them, and re-layouts  13.7 us (19%)
  starting transfers between devices  7.95 us (11%)
  waiting for transfers between devices  4.72 us (7%)
  between operations  2.82 us (4%)
  other arithmetic  1.37 us (2%)
    pallas_call x1, Pallas kernels, per_device(): pl.pallas_call(functools.partial(reduce_kernel, n_x, n_lon), out_shape=ja...  30.2 us
    pallas_call x1, Pallas kernels, per_device(): pl.pallas_call(functools.partial(compute_kernel, rows, cols, total_rows,...  9.41 us
    unnamed x27, local copies, waits for them, and re-layouts  8.94 us
    ppermute x2, starting transfers between devices, passed_along(): return lax.ppermute(value, axis, pairs)  4.95 us
    ppermute x2, waiting for transfers between devices, passed_along(): return lax.ppermute(value, axis, pairs)  4.72 us
    ppermute x1, starting transfers between devices, shifted_2(): return lax.ppermute(block, axis, route)  2.99 us
  transfers between devices with their start and end apart: 3, of which 2 were waited for; matrix products, arithmetic and copies ran while one was open for 5% of the time, Pallas kernels for 0%

profile of v1, /device:TPU:0, one launch (start us, length us, event | category | flops | bytes accessed | tf_op | source)
XLA Modules:
  0.0 70.2 jit_solution(15201778010996584759)
XLA Ops:
  0.6 2.1 %copy.93 = bf16[192,16,256]{2,0,1:T(8,128)(2,1)S(1)} copy(bf16[192,16,256]{2,1,0:T(8,128)(2,1)} %param.9) | data formatting | bytes 3145728 | tf_op args[0]
  2.7 0.7 slice_bitcast_fusion
  3.4 3.0 %collective-permute-start.1 = (bf16[192,256]{1,0:T(8,128)(2,1)}, bf16[192,256]{1,0:T(8,128)(2,1)}, u32[]{:S(2)}, u32[]{:S(2)}) collective-permute-start(bf16[192,256]{1,0:T(8,128)(2,1)} %get-tuple-element.39), channel_id=1, source_target_pairs={{0,4},{4,8},{8,12},{1,5},{5,9},{9,13},{2,6},{6,10},{10,14},{3,7},{... | collective-permute-start | bytes 294920 | tf_op jit(solution)/shard_map/ppermute | solution.py:31
  6.4 3.4 %collective-permute-start = (bf16[192,256]{1,0:T(8,128)(2,1)}, bf16[192,256]{1,0:T(8,128)(2,1)}, u32[]{:S(2)}, u32[]{:S(2)}) collective-permute-start(bf16[192,256]{1,0:T(8,128)(2,1)} %get-tuple-element.40), channel_id=1, source_target_pairs={{0,2},{1,3},{2,0},{3,1},{4,6},{5,7},{6,4},{7,5},{8,10},{9,11},{10,... | collective-permute-start | bytes 294920 | tf_op jit(solution)/shard_map/ppermute | solution.py:25
  9.8 0.3 slice.52
  10.1 1.2 %copy.70 = bf16[192,16,1]{1,0,2:T(8,128)(2,1)S(1)} copy(bf16[192,16,1]{2,1,0:T(8,128)(2,1)S(1)} %slice.52) | data formatting | bytes 12288
  11.3 4.0 %collective-permute-done = bf16[192,256]{1,0:T(8,128)(2,1)} collective-permute-done((bf16[192,256]{1,0:T(8,128)(2,1)}, bf16[192,256]{1,0:T(8,128)(2,1)}, u32[]{:S(2)}, u32[]{:S(2)}) %collective-permute-start) | collective-permute-done | bytes 98336 | tf_op jit(solution)/shard_map/ppermute | solution.py:25
  15.4 0.9 %broadcast_select_fusion.top = bf16[192,256]{1,0:T(8,128)(2,1)S(1)} fusion(bf16[192,256]{1,0:T(8,128)(2,1)} %collective-permute-done, bf16[192,256]{1,0:T(8,128)(2,1)} %collective-permute-done.1, pred[]{:T(512)S(6)} %eq.3), kind=kLoop, calls=%fused_computation.11 | loop fusion | flops 49152 | bytes 294913 | tf_op jit(solution)/shard_map/jit(_where)/select_n | solution.py:315
  16.5 1.5 %collective-permute-start.2 = (bf16[192,17]{1,0:T(8,128)(2,1)S(1)}, bf16[192,17]{1,0:T(8,128)(2,1)S(1)}, u32[]{:S(2)}, u32[]{:S(2)}) collective-permute-start(bf16[192,17]{1,0:T(8,128)(2,1)S(1)} %pad_maximum_fusion), channel_id=1, source_target_pairs={{0,1},{1,2},{2,3},{3,0},{4,5},{5,6},{6,7},{7,4},{8,9},{9,10},{10,1... | collective-permute-start | bytes 19592 | tf_op jit(solution)/shard_map/ppermute | solution.py:25
  18.0 0.6 fusion.4
  20.8 1.1 %copy.62.ew = bf16[768,192]{1,0:T(8,128)(2,1)S(1)} copy(bf16[768,192]{0,1:T(8,128)(2,1)} %param.12) | data formatting | bytes 589824 | tf_op args[3]
  22.2 0.7 collective-permute-done.2
  22.9 1.0 %copy-done.1 = bf16[192,768]{1,0:T(8,128)(2,1)S(1)} copy-done((bf16[192,768]{1,0:T(8,128)(2,1)S(1)}, bf16[192,768]{1,0:T(8,128)(2,1)}, u32[]{:S(2)}) %copy-start.1) | copy-done | bytes 294936
  23.9 9.4 %segment.1 = (bf16[8,192,128]{2,1,0:T(8,128)(2,1)S(1)}, bf16[2816,128]{1,0:T(8,128)(2,1)S(1)}) custom-call(s32[1]{0:T(128)} %bitcast.2.salt_ref, bf16[16,192,256]{2,1,0:T(8,128)(2,1)S(1)} %bitcast.55, bf16[192,256]{1,0:T(8,128)(2,1)S(1)} %broadcast_select_fusion.top, bf16[192,128]{1,0:T(8,128)(2,1)S(1)} %pad.4.west, bf16[192,1728]{1,0:T(8,128)(2,1)S(1)} %copy-done, ...), custom_call_target="tpu_custom_call" | custom-call | tf_op jit(solution)/shard_map/segment/pallas_call | solution.py:327
  33.3 30.2 %gradient_sum.1 = bf16[2,2816,128]{2,1,0:T(8,128)(2,1)S(1)} custom-call(bf16[2816,128]{1,0:T(8,128)(2,1)S(1)} %get-tuple-element.10.payload), custom_call_target="tpu_custom_call" | custom-call | tf_op jit(solution)/shard_map/gradient_sum/pallas_call | solution.py:364
  63.8 0.6 slice.71
  64.4 1.0 %copy.69 = bf16[1,192,8,128]{3,2,1,0:T(8,128)(2,1)} copy(bf16[1,192,8,128]{3,1,2,0:T(8,128)(2,1)S(1)} %bitcast.57) | data formatting | bytes 786432
  65.4 0.7 reshape.44
  66.1 0.4 copy.65
  66.5 0.5 copy.89
  67.0 0.9 %slice_reduce_fusion = f32[192]{0:T(256)} fusion(f32[192,1792]{1,0:T(8,128)S(1)} %bitcast.64), kind=kLoop, calls=%fused_computation.8 | loop fusion | bytes 1536 | tf_op jit(solution)/shard_map/slice | solution.py:387
  67.9 0.4 fusion
  68.3 0.9 %copy.90 = f32[24,8,6,128]{3,1,2,0:T(8,128)} copy(f32[24,8,6,128]{3,2,1,0:T(8,128)S(1)} %bitcast.60) | data formatting | bytes 1179648
  69.2 0.9 %copy.91 = f32[24,8,6,128]{3,1,2,0:T(8,128)} copy(f32[24,8,6,128]{3,2,1,0:T(8,128)S(1)} %bitcast.59) | data formatting | bytes 1179648
  (32 shorter events, 1.0 us)
Async XLA Ops:
  0.6 9.2 %copy-start.2 = (bf16[192,16,256]{2,1,0:T(8,128)(2,1)S(1)}, bf16[192,16,256]{2,1,0:T(8,128)(2,1)}, u32[]{:S(2)}) copy-start(bf16[192,16,256]{2,1,0:T(8,128)(2,1)} %param.9) | copy-start | bytes 4718596
  3.4 8.0 %collective-permute-start.1 = (bf16[192,256]{1,0:T(8,128)(2,1)}, bf16[192,256]{1,0:T(8,128)(2,1)}, u32[]{:S(2)}, u32[]{:S(2)}) collective-permute-start(bf16[192,256]{1,0:T(8,128)(2,1)} %get-tuple-element.39), channel_id=1, source_target_pairs={{0,4},{4,8},{8,12},{1,5},{5,9},{9,13},{2,6},{6,10},{10,14},{3,7},{... | collective-permute-start | bytes 294920 | tf_op jit(solution)/shard_map/ppermute | solution.py:31
  6.4 9.0 %collective-permute-start = (bf16[192,256]{1,0:T(8,128)(2,1)}, bf16[192,256]{1,0:T(8,128)(2,1)}, u32[]{:S(2)}, u32[]{:S(2)}) collective-permute-start(bf16[192,256]{1,0:T(8,128)(2,1)} %get-tuple-element.40), channel_id=1, source_target_pairs={{0,2},{1,3},{2,0},{3,1},{4,6},{5,7},{6,4},{7,5},{8,10},{9,11},{10,... | collective-permute-start | bytes 294920 | tf_op jit(solution)/shard_map/ppermute | solution.py:25
  9.8 8.2 %copy-start.6 = (s32[2]{0:T(128)S(1)}, s32[2]{0:T(128)}, u32[]{:S(2)}) copy-start(s32[2]{0:T(128)} %param.17) | copy-start | bytes 28
  9.8 10.7 %copy-start.7 = (f32[192]{0:T(256)S(1)}, f32[192]{0:T(256)}, u32[]{:S(2)}) copy-start(f32[192]{0:T(256)} %param.11) | copy-start | bytes 2308
  9.8 10.9 %copy-start.8 = (f32[192]{0:T(256)S(1)}, f32[192]{0:T(256)}, u32[]{:S(2)}) copy-start(f32[192]{0:T(256)} %param.15) | copy-start | bytes 2308
  10.1 11.9 %copy-start.5 = (f32[768]{0:T(1024)S(1)}, f32[768]{0:T(1024)}, u32[]{:S(2)}) copy-start(f32[768]{0:T(1024)} %param.13) | copy-start | bytes 9220
  10.1 12.0 %copy-start.4 = (bf16[192,8,128]{2,1,0:T(8,128)(2,1)S(1)}, bf16[192,8,128]{2,1,0:T(8,128)(2,1)}, u32[]{:S(2)}) copy-start(bf16[192,8,128]{2,1,0:T(8,128)(2,1)} %param.16) | copy-start | bytes 1179652
  11.3 11.6 %copy-start = (bf16[192,1728]{1,0:T(8,128)(2,1)S(1)}, bf16[192,1728]{1,0:T(8,128)(2,1)}, u32[]{:S(2)}) copy-start(bf16[192,1728]{1,0:T(8,128)(2,1)} %cw.1) | copy-start | bytes 1990660
  16.5 6.4 %collective-permute-start.2 = (bf16[192,17]{1,0:T(8,128)(2,1)S(1)}, bf16[192,17]{1,0:T(8,128)(2,1)S(1)}, u32[]{:S(2)}, u32[]{:S(2)}) collective-permute-start(bf16[192,17]{1,0:T(8,128)(2,1)S(1)} %pad_maximum_fusion), channel_id=1, source_target_pairs={{0,1},{1,2},{2,3},{3,0},{4,5},{5,6},{6,7},{7,4},{8,9},{9,10},{10,1... | collective-permute-start | bytes 19592 | tf_op jit(solution)/shard_map/ppermute | solution.py:25
  22.9 1.0 %copy-start.1 = (bf16[192,768]{1,0:T(8,128)(2,1)S(1)}, bf16[192,768]{1,0:T(8,128)(2,1)}, u32[]{:S(2)}) copy-start(bf16[192,768]{1,0:T(8,128)(2,1)} %pw.1) | copy-start | bytes 884740
  67.0 2.2 %copy-start.3 = (f32[24,8,14,128]{3,1,2,0:T(8,128)}, f32[24,8,14,128]{3,1,2,0:T(8,128)S(1)}, u32[]{:S(2)}) copy-start(f32[24,8,14,128]{3,1,2,0:T(8,128)S(1)} %copy.89) | copy-start | bytes 4128772

commit v2 on v1

--- a/solution.py
+++ b/solution.py
@@ -15,20 +15,9 @@
 ROOT = 0.7978845608028654
 CUBIC = 0.044715
 MESH = pl.DeviceIdType.MESH
+FLOWS = 3
 BF = jnp.bfloat16
 F32 = jnp.float32
-
-
-def passed_along(value, axis, steps):
-    count = lax.axis_size(axis)
-    pairs = [(source, (source + steps) % count) for source in range(count)]
-    return lax.ppermute(value, axis, pairs)
-
-
-def shifted_2(block, axis, distance):
-    devices = range(lax.axis_size(axis))
-    route = [(i - distance, i) for i in devices if i - distance in devices]
-    return lax.ppermute(block, axis, route)
 
 
 def shifted(number, places):
@@ -74,6 +63,7 @@
     xt,
     top,
     west,
+    corner,
     cw,
     cb,
     ew,
@@ -91,7 +81,7 @@
     dp_s,
 ):
     channels, taps = cw.shape
-    hidden = ew.shape[0]
+    hidden = ew.shape[1]
     cells = rows * cols
     pad_taps = patches.shape[0]
     is_encoder = lax.axis_index("pipe") == 0
@@ -106,12 +96,13 @@
     select = jnp.where(source == wanted, 1.0, 0.0).astype(BF)
     edge_row = lax.broadcasted_iota(jnp.int32, (128, cols), 0)
     edge_col = lax.broadcasted_iota(jnp.int32, (128, cols), 1)
-    west_edge = west[...]
     for q in range(2 * rows + 1):
         line = top[...] if q == 0 else xt[q - 1]
         split = dot(line, select, NN)
-        pick = jnp.where((edge_row == q) & (edge_col == 0), 1.0, 0.0).astype(BF)
-        first = (split[:, :cols] + dot(west_edge, pick, NN)).astype(BF)
+        lane = 127 if q == 0 else q - 1
+        edge = corner[...] if q == 0 else west[...]
+        pick = jnp.where((edge_row == lane) & (edge_col == 0), 1.0, 0.0).astype(BF)
+        first = (split[:, :cols] + dot(edge, pick, NN)).astype(BF)
         parts = [first, split[:, cols : 2 * cols].astype(BF), split[:, 2 * cols :].astype(BF)]
         places = [(1, q // 2)] if q % 2 else [(a, q // 2 - a // 2) for a in (0, 2)]
         for a, r in places:
@@ -136,7 +127,7 @@
         pre = dot(cw[...], patches[:taps, here], NN) + cb[...]
         value, pre_slope = gelu_both(pre)
         encoded = (value * keep).astype(BF)
-        inner = dot(ew[...], encoded, NN) + eb[...]
+        inner = dot(ew[...], encoded, TN) + eb[...]
         activated, slope = gelu_both(inner)
         activated = activated.astype(BF)
         scaled = jnp.concatenate([cot[2 * j], cot[2 * j + 1]], axis=1).astype(F32) * scale
@@ -147,7 +138,7 @@
         def encoder_part(sums=sums):
             field_out[2 * j] = encoded[:, :cols]
             field_out[2 * j + 1] = encoded[:, cols:]
-            d_encoded = (scaled + dot(ew[...], d_half, TN)).astype(BF)
+            d_encoded = (scaled + dot(ew[...], d_half, NN)).astype(BF)
             d_pre = d_encoded.astype(F32) * keep * pre_slope
             dp_s[:, here] = d_pre.astype(BF)
             act_s[0:channels, j * 128 : j * 128 + 128] = jnp.sum(d_pre, axis=1, keepdims=True) + jnp.zeros(
@@ -203,18 +194,110 @@
     payload[blocks * channels :, :] = jnp.zeros((total_rows - blocks * channels, 128), BF)
 
 
-def reduce_kernel(
-    n_x, n_z, payload, out, buf1, s1, buf2, s2, buf3, send, recv
-):
+def halo_kernel(n_lat, n_lon, xt, top, west, corner, edge, send, recv):
+    pipe = lax.axis_index("pipe")
+    lat = lax.axis_index("lat")
+    lon = lax.axis_index("lon")
+    last = xt.shape[0] - 1
+    width = xt.shape[2]
+    away = n_lon // 2
+    is_first = lat == 0
+    north = jnp.where(is_first, 0, lat - 1)
+    turn = jnp.where(is_first, away, 0)
+    has_south = lat < n_lat - 1
+    sources = [
+        (pipe, lat, (lon + n_lon - 1) % n_lon),
+        (pipe, north, (lon + n_lon - turn) % n_lon),
+        (pipe, north, (lon + n_lon - turn - 1 + n_lon) % n_lon),
+    ]
+    barrier = pltpu.get_barrier_semaphore()
+    for peer in sources:
+        pl.semaphore_signal(barrier, inc=1, device_id=peer, device_id_type=MESH)
+    sends = 1 + jnp.where(has_south, 2, 0) + jnp.where(is_first, 2, 0)
+
+    def copy(src, dst, i, j, peer):
+        return pltpu.make_async_remote_copy(
+            src_ref=src,
+            dst_ref=dst,
+            send_sem=send.at[i],
+            recv_sem=recv.at[j],
+            device_id=peer,
+            device_id_type=MESH,
+        )
+
+    right = pl.ds(width - 128, 128)
+
+    def pair(row, i, lat_to, lon_to):
+        return [
+            copy(xt.at[row], top, i, 0, (pipe, lat_to, lon_to % n_lon)),
+            copy(xt.at[row, :, right], corner, i + 1, 1, (pipe, lat_to, (lon_to + 1) % n_lon)),
+        ]
+
+    south = pair(last, 0, jnp.where(has_south, lat + 1, lat), lon)
+    pole = pair(0, 2, lat, lon + away)
+    pl.semaphore_wait(barrier, sends)
+
+    @pl.when(has_south)
+    def _():
+        for item in south:
+            item.start()
+
+    @pl.when(is_first)
+    def _():
+        for item in pole:
+            item.start()
+
+    row_id = lax.broadcasted_iota(jnp.int32, (128, 128), 0)
+    col_id = lax.broadcasted_iota(jnp.int32, (128, 128), 1)
+    total = None
+    for q in range(last + 1):
+        pick = jnp.where((row_id == 127) & (col_id == q), 1.0, 0.0).astype(BF)
+        term = dot(xt[q, :, width - 128 :], pick, NN)
+        total = term if total is None else total + term
+    edge[...] = total.astype(BF)
+    east = copy(edge, west, 4, 2, (pipe, lat, (lon + 1) % n_lon))
+    east.start()
+    for item in pole:
+        item.wait_recv()
+    east.wait()
+
+    @pl.when(has_south)
+    def _():
+        for item in south:
+            item.wait_send()
+
+    @pl.when(is_first)
+    def _():
+        for item in pole:
+            item.wait_send()
+
+
+def finish_kernel(taps, hidden, gathered, conv, project, expand, conv_bias, biases):
+    channels = conv.shape[0]
+    blocks = -(-(taps + 1) // 128)
+    per = hidden // 128
+    for k in range(blocks):
+        width = min(128, taps - 128 * k)
+        block = gathered[0, k * channels : (k + 1) * channels, :]
+        conv[:, 128 * k : 128 * k + width] = block[:, :width].astype(F32)
+        if k == blocks - 1:
+            pick = lax.broadcasted_iota(jnp.int32, (8, 128), 1) == taps - 128 * k
+            conv_bias[...] = dot(jnp.where(pick, 1.0, 0.0).astype(BF), block, NT)
+    for k in range(per):
+        here = slice(128 * k, 128 * k + 128)
+        project[:, here] = gathered[1, k * channels : (k + 1) * channels, :].astype(F32)
+        expand[:, here] = gathered[1, (per + k) * channels : (per + k + 1) * channels, :].astype(F32)
+    block = gathered[1, 2 * per * channels : (2 * per + 1) * channels, :]
+    pick = lax.broadcasted_iota(jnp.int32, (8, 128), 1) == lax.broadcasted_iota(jnp.int32, (8, 128), 0)
+    biases[...] = dot(jnp.where(pick, 1.0, 0.0).astype(BF), block, NT)
+
+
+def reduce_kernel(n_x, n_z, flows, payload, out, buf1, s1, buf2, s2, buf3, send, recv):
     pipe = lax.axis_index("pipe")
     lat = lax.axis_index("lat")
     z = lax.axis_index("lon")
     x = lat // 2
     core = lat % 2
-    total_rows = payload.shape[0]
-    half = total_rows // 2
-    part = half // n_x
-    own = part // n_z
     twin = (pipe, 2 * x + 1 - core, z)
 
     def z_peer(d):
@@ -251,38 +334,80 @@
     def at(start, size):
         return pl.ds(pl.multiple_of(start, 16), size)
 
-    push(payload.at[at((1 - core) * half, half)], buf1, twin).wait_recv()
-    s1[...] = (payload[at(core * half, half), :].astype(F32) + buf1[...].astype(F32)).astype(BF)
-
-    arrivals = []
-    for d in range(1, n_x):
-        arrivals.append(push(s1.at[at(((x + d) % n_x) * part, part)], buf2.at[d - 1], xp_peer(d, 0)))
-    total = s1[at(x * part, part), :].astype(F32)
-    for d in range(1, n_x):
-        arrivals[d - 1].wait_recv()
-        total = total + buf2[d - 1].astype(F32)
-    s2[...] = total.astype(BF)
-
-    arrivals = []
-    for d in range(1, n_z):
-        arrivals.append(push(s2.at[at(((z + d) % n_z) * own, own)], buf3.at[d - 1], z_peer(d)))
-    total = s2[at(z * own, own), :].astype(F32)
-    for d in range(1, n_z):
-        arrivals[d - 1].wait_recv()
-        total = total + buf3[d - 1].astype(F32)
-    mine = out.at[pipe, at(core * half + x * part + z * own, own)]
-    mine[...] = total.astype(BF)
-
-    arrivals = [push(mine, mine, z_peer(d)) for d in range(1, n_z)]
-    for copy in arrivals:
-        copy.wait_recv()
-    column = out.at[pipe, at(core * half + x * part, part)]
-    arrivals = [push(column, column, xp_peer(*o)) for o in others]
-    final = [push(column, column, twin)]
-    for (dx, dp), copy in zip(others, arrivals):
-        copy.wait_recv()
-        block = out.at[(pipe + dp) % 2, at(core * half + ((x - dx + n_x) % n_x) * part, part)]
-        final.append(push(block, block, twin))
+    halves = [size // 2 for _, size in flows]
+    parts = [half // n_x for half in halves]
+    owns = [part // n_z for part in parts]
+    ids = range(len(flows))
+
+    firsts = []
+    for f in ids:
+        start = flows[f][0]
+        half = halves[f]
+        source = payload.at[at(start + (1 - core) * half, half)]
+        firsts.append(push(source, buf1.at[f, pl.ds(0, half)], twin))
+
+    seconds = []
+    for f in ids:
+        half, part = halves[f], parts[f]
+        firsts[f].wait_recv()
+        kept = payload[at(flows[f][0] + core * half, half), :]
+        s1[f, :half] = (kept.astype(F32) + buf1[f, :half].astype(F32)).astype(BF)
+        seconds.append(
+            [
+                push(
+                    s1.at[f, at(((x + d) % n_x) * part, part)],
+                    buf2.at[f, d - 1, pl.ds(0, part)],
+                    xp_peer(d, 0),
+                )
+                for d in range(1, n_x)
+            ]
+        )
+
+    thirds = []
+    for f in ids:
+        part, own = parts[f], owns[f]
+        total = s1[f, at(x * part, part), :].astype(F32)
+        for d in range(1, n_x):
+            seconds[f][d - 1].wait_recv()
+            total = total + buf2[f, d - 1, :part].astype(F32)
+        s2[f, :part] = total.astype(BF)
+        thirds.append(
+            [
+                push(
+                    s2.at[f, at(((z + d) % n_z) * own, own)],
+                    buf3.at[f, d - 1, pl.ds(0, own)],
+                    z_peer(d),
+                )
+                for d in range(1, n_z)
+            ]
+        )
+
+    fourths = []
+    for f in ids:
+        part, own = parts[f], owns[f]
+        total = s2[f, at(z * own, own), :].astype(F32)
+        for d in range(1, n_z):
+            thirds[f][d - 1].wait_recv()
+            total = total + buf3[f, d - 1, :own].astype(F32)
+        place = at(flows[f][0] + core * halves[f] + x * part + z * own, own)
+        mine = out.at[pipe, place]
+        mine[...] = total.astype(BF)
+        fourths.append([push(mine, mine, z_peer(d)) for d in range(1, n_z)])
+
+    fifths = []
+    final = []
+    for f in ids:
+        for copy in fourths[f]:
+            copy.wait_recv()
+        column = out.at[pipe, at(flows[f][0] + core * halves[f] + x * parts[f], parts[f])]
+        fifths.append([push(column, column, xp_peer(*o)) for o in others])
+        final.append(push(column, column, twin))
+    for f in ids:
+        for (dx, dp), copy in zip(others, fifths[f]):
+            copy.wait_recv()
+            start = flows[f][0] + core * halves[f] + ((x - dx + n_x) % n_x) * parts[f]
+            block = out.at[(pipe + dp) % 2, at(start, parts[f])]
+            final.append(push(block, block, twin))
     for copy in final:
         copy.wait_recv()
     for copy in started:
@@ -310,12 +435,6 @@
     n_lon = lax.axis_size("lon")
     scale = float(cells * n_lat * n_lon) ** (-0.5)
 
-    from_above = shifted_2(field[:, row_count - 1, :], "lat", 1)
-    mirrored = passed_along(field[:, 0, :], "lon", n_lon // 2)
-    top = jnp.where(lax.axis_index("lat") == 0, mirrored, from_above)
-    edge = jnp.concatenate([top[:, col_count - 1 :], field[:, :, col_count - 1]], axis=1)
-    west = passed_along(edge, "lon", 1)
-    west = jnp.pad(west, ((0, 0), (0, 128 - row_count - 1)))
     salt = scramble(dropout_key[0] + scramble(dropout_key[1])).reshape(1)
 
     pad_taps = -(-(taps + 1) // 128) * 128
@@ -324,13 +443,31 @@
     total_rows = -(-(blocks * channels) // unit) * unit
     vmem = pl.BlockSpec(memory_space=pltpu.VMEM)
     smem = pl.BlockSpec(memory_space=pltpu.SMEM)
+    turned = jnp.transpose(field, (1, 0, 2))
+    row_shape = jax.ShapeDtypeStruct((channels, col_count), BF)
+    edge_shape = jax.ShapeDtypeStruct((channels, 128), BF)
+    top, west, corner = pl.pallas_call(
+        functools.partial(halo_kernel, n_lat, n_lon),
+        out_shape=(row_shape, edge_shape, edge_shape),
+        in_specs=[vmem],
+        out_specs=(vmem, vmem, vmem),
+        scratch_shapes=[
+            pltpu.VMEM((channels, 128), BF),
+            pltpu.SemaphoreType.DMA((5,)),
+            pltpu.SemaphoreType.DMA((3,)),
+        ],
+        compiler_params=pltpu.CompilerParams(
+            collective_id=1, has_side_effects=True, vmem_limit_bytes=16 * 1024 * 1024
+        ),
+        name="halo",
+    )(turned)
     field_out, payload = pl.pallas_call(
         functools.partial(compute_kernel, rows, cols, total_rows, scale),
         out_shape=(
             jax.ShapeDtypeStruct((rows, channels, cols), BF),
             jax.ShapeDtypeStruct((total_rows, 128), BF),
         ),
-        in_specs=[smem] + [vmem] * 10,
+        in_specs=[smem] + [vmem] * 11,
         out_specs=(vmem, vmem),
         scratch_shapes=[
             pltpu.VMEM((pad_taps, cells), BF),
@@ -344,12 +481,13 @@
         name="segment",
     )(
         salt,
-        jnp.transpose(field, (1, 0, 2)),
+        turned,
         top,
         west,
+        corner,
         conv_weight,
         conv_bias[:, None],
-        expand_weight,
+        expand_weight.T,
         expand_bias[:, None],
         project_weight,
         project_bias[:, None],
@@ -357,21 +495,25 @@
     )
 
     n_x = n_lat // 2
-    half = total_rows // 2
+    units = total_rows // unit
+    count = min(FLOWS, units)
+    sizes = [(units // count + (1 if f < units % count else 0)) * unit for f in range(count)]
+    flows = [(sum(sizes[:f]), sizes[f]) for f in range(count)]
+    half = sizes[0] // 2
     part = half // n_x
     own = part // n_lon
-    copies = 1 + (n_x - 1) + 2 * (n_lon - 1) + 2 * (2 * n_x - 1) + 1
+    copies = count * (1 + (n_x - 1) + 2 * (n_lon - 1) + 2 * (2 * n_x - 1) + 1)
     gathered = pl.pallas_call(
-        functools.partial(reduce_kernel, n_x, n_lon),
+        functools.partial(reduce_kernel, n_x, n_lon, flows),
         out_shape=jax.ShapeDtypeStruct((2, total_rows, 128), BF),
         in_specs=[vmem],
         out_specs=vmem,
         scratch_shapes=[
-            pltpu.VMEM((half, 128), BF),
-            pltpu.VMEM((half, 128), BF),
-            pltpu.VMEM((n_x - 1, part, 128), BF),
-            pltpu.VMEM((part, 128), BF),
-            pltpu.VMEM((n_lon - 1, own, 128), BF),
+            pltpu.VMEM((count, half, 128), BF),
+            pltpu.VMEM((count, half, 128), BF),
+            pltpu.VMEM((count, n_x - 1, part, 128), BF),
+            pltpu.VMEM((count, part, 128), BF),
+            pltpu.VMEM((count, n_lon - 1, own, 128), BF),
             pltpu.SemaphoreType.DMA((copies,)),
             pltpu.SemaphoreType.DMA((copies,)),
         ],
@@ -381,16 +523,20 @@
         name="gradient_sum",
     )(payload)
 
-    used = gathered[:, : blocks * channels].reshape(2, blocks, channels, 128)
-    wide = used[0].transpose(1, 0, 2).reshape(channels, pad_taps).astype(F32)
-    conv_grad = wide[:, :taps]
-    conv_bias_grad = wide[:, taps]
-    per = hidden // 128
-    project_grad = used[1, :per].transpose(1, 0, 2).reshape(channels, hidden).astype(F32)
-    expand_grad = used[1, per : 2 * per].transpose(0, 2, 1).reshape(hidden, channels).astype(F32)
-    biases = used[1, 2 * per].astype(F32)
-    project_bias_grad = biases[:, 0]
-    expand_bias_grad = biases[:, 1 : 1 + hidden // channels].T.reshape(hidden)
+    wide = jax.ShapeDtypeStruct((channels, hidden), F32)
+    short = jax.ShapeDtypeStruct((8, channels), F32)
+    conv_grad, project_grad, expand_turned, conv_rows, bias_rows = pl.pallas_call(
+        functools.partial(finish_kernel, taps, hidden),
+        out_shape=(jax.ShapeDtypeStruct((channels, taps), F32), wide, wide, short, short),
+        in_specs=[vmem],
+        out_specs=(vmem,) * 5,
+        compiler_params=pltpu.CompilerParams(vmem_limit_bytes=32 * 1024 * 1024),
+        name="widen",
+    )(gathered)
+    expand_grad = expand_turned.T
+    conv_bias_grad = conv_rows[0]
+    project_bias_grad = bias_rows[0]
+    expand_bias_grad = bias_rows[1 : 1 + hidden // channels].reshape(hidden)
     section_fields = jnp.transpose(field_out, (1, 0, 2))[None]
     return (
         section_fields,

time: 70.4 us -> 59.7 us (0.85)
  starting transfers between devices: 7.95 us -> 0 us
  Pallas kernels: 39.6 us -> 47.2 us
  waiting for transfers between devices: 4.72 us -> 0 us
  local copies, waits for them, and re-layouts: 13.7 us -> 9.56 us
  other arithmetic: 1.37 us -> 0 us
    ppermute x3 -> x0, starting transfers between devices: 7.95 us -> none  [the longest x2 4.95 us: passed_along(): return lax.ppermute(value, axis, pairs)]
    pallas_call x1 -> x3, Pallas kernels: 30.2 us -> 38 us  [the longest x1 25.1 us: per_device(): pl.pallas_call(functools.partial(reduce_kernel, n_x, n_lon, flows), out_s...]
    unnamed x27 -> x9, local copies, waits for them, and re-layouts: 8.94 us -> 4.01 us
    ppermute x3 -> x0, waiting for transfers between devices: 4.72 us -> none  [the longest x2 4.72 us: passed_along(): return lax.ppermute(value, axis, pairs)]
    select_n x1 -> x0, other arithmetic: 0.91 us -> none  [per_device(): top = jnp.where(lax.axis_index('lat') == 0, mirrored, from_above)]
    slice x8 -> x3, local copies, waits for them, and re-layouts: 2.03 us -> 1.13 us  [the longest x1 0.56 us: per_device(): conv_bias_grad = conv_rows[0]]
    slice x1, local copies, waits for them, and re-layouts: 0.58 us -> 1.31 us  [per_device(): salt = scramble(dropout_key[0] + scramble(dropout_key[1])).reshape(1)]
  transfers between devices with their start and end apart: 3 -> 0, of which waited for: 2 -> 0; matrix products, arithmetic and copies ran while one was open for 5% -> 0% of each run, Pallas kernels for 0% -> 0%
where the time goes in v2:
time: 59.7 us; the launch traced here: 59.4 us
  Pallas kernels  47.2 us (79%)
  local copies, waits for them, and re-layouts  9.56 us (16%)
  between operations  2.69 us (5%)
    pallas_call x1, Pallas kernels, per_device(): pl.pallas_call(functools.partial(reduce_kernel, n_x, n_lon, flows), out_s...  25.1 us
    pallas_call x1, Pallas kernels, per_device(): pl.pallas_call(functools.partial(halo_kernel, n_lat, n_lon), out_shape=(r...  11.4 us
    pallas_call x1, Pallas kernels, per_device(): pl.pallas_call(functools.partial(compute_kernel, rows, cols, total_rows,...  9.17 us
    unnamed x9, local copies, waits for them, and re-layouts  4.01 us
    pallas_call x1, Pallas kernels, per_device(): pl.pallas_call(functools.partial(finish_kernel, taps, hidden), out_shape=...  1.52 us
    slice x1, local copies, waits for them, and re-layouts, per_device(): salt = scramble(dropout_key[0] + scramble(dropout_key[1])).reshape(1)  1.31 us

profile of v2, /device:TPU:0, one launch (start us, length us, event | category | flops | bytes accessed | tf_op | source)
XLA Modules:
  0.0 59.4 jit_solution(2178041417344825053)
XLA Ops:
  0.6 1.3 %fusion = (s32[1]{0:T(128)}, s32[1]{0:T(128)}) fusion(s32[2]{0:T(128)} %param.17), kind=kLoop, calls=%fused_computation.2 | loop fusion | bytes 16 | tf_op jit(solution)/shard_map/slice | solution.py:438
  3.9 0.8 %copy.21.cb = f32[192,1]{1,0:T(8,128)S(1)} copy(f32[192,1]{0,1:T(1,128)} %bitcast.23) | data formatting | bytes 1536 | tf_op jit(solution)/shard_map/broadcast_in_dim | solution.py:489
  4.7 0.8 %copy.23.pb = f32[192,1]{1,0:T(8,128)S(1)} copy(f32[192,1]{0,1:T(1,128)} %bitcast.24) | data formatting | bytes 1536 | tf_op jit(solution)/shard_map/broadcast_in_dim | solution.py:493
  5.5 0.8 %broadcast_in_dim.16.eb = f32[768,1]{1,0:T(8,128)S(1)} reshape(f32[768]{0:T(1024)} %param.13) | data formatting | bytes 6144 | tf_op jit(solution)/shard_map/broadcast_in_dim | solution.py:491
  6.4 1.1 %copy.28 = bf16[192,8,128]{2,0,1:T(8,128)(2,1)S(1)} copy(bf16[192,8,128]{2,1,0:T(8,128)(2,1)} %param.16) | data formatting | bytes 786432 | tf_op args[7]
  7.4 1.9 %copy.27 = bf16[192,16,256]{2,0,1:T(8,128)(2,1)S(1)} copy(bf16[192,16,256]{2,1,0:T(8,128)(2,1)} %param.9) | data formatting | bytes 3145728 | tf_op args[0]
  9.4 0.0 copy-start
  9.4 0.0 copy-start.1
  9.4 0.0 copy-start.2
  9.4 11.4 %halo.1 = (bf16[192,256]{1,0:T(8,128)(2,1)S(1)}, bf16[192,128]{1,0:T(8,128)(2,1)S(1)}, bf16[192,128]{1,0:T(8,128)(2,1)S(1)}) custom-call(bf16[16,192,256]{2,1,0:T(8,128)(2,1)S(1)} %bitcast.18), custom_call_target="tpu_custom_call" | custom-call | tf_op jit(solution)/shard_map/halo/pallas_call | solution.py:449
  20.8 0.0 copy-done
  20.8 0.0 copy-done.1
  20.8 0.0 copy-done.2
  20.8 9.2 %segment.1 = (bf16[8,192,128]{2,1,0:T(8,128)(2,1)S(1)}, bf16[2816,128]{1,0:T(8,128)(2,1)S(1)}) custom-call(s32[1]{0:T(128)} %bitcast.2.salt_ref, bf16[16,192,256]{2,1,0:T(8,128)(2,1)S(1)} %bitcast.19, bf16[192,256]{1,0:T(8,128)(2,1)S(1)} %get-tuple-element.17.top, bf16[192,128]{1,0:T(8,128)(2,1)S(1)} %get-tuple-element.18.west, ...), custom_call_target="tpu_custom_call" | custom-call | tf_op jit(solution)/shard_map/segment/pallas_call | solution.py:464
  30.0 1.0 %copy.24 = bf16[1,192,8,128]{3,2,1,0:T(8,128)(2,1)} copy(bf16[1,192,8,128]{3,1,2,0:T(8,128)(2,1)S(1)} %bitcast.21) | data formatting | bytes 786432
  31.0 25.1 %gradient_sum.1.gathered = bf16[2,2816,128]{2,1,0:T(8,128)(2,1)S(1)} custom-call(bf16[2816,128]{1,0:T(8,128)(2,1)S(1)} %get-tuple-element.21.payload), custom_call_target="tpu_custom_call" | custom-call | tf_op jit(solution)/shard_map/gradient_sum/pallas_call | solution.py:506
  56.1 1.5 %widen.1 = (f32[192,1728]{1,0:T(8,128)}, f32[192,768]{1,0:T(8,128)}, f32[192,768]{1,0:T(8,128)}, f32[8,192]{1,0:T(8,128)S(1)}, f32[8,192]{1,0:T(8,128)S(1)}) custom-call(bf16[2,2816,128]{2,1,0:T(8,128)(2,1)S(1)} %gradient_sum.1.gathered), custom_call_target="tpu_custom_call" | custom-call | tf_op jit(solution)/shard_map/widen/pallas_call | solution.py:528
  57.6 0.6 slice.17
  58.2 0.6 slice.19
  58.8 0.7 %reshape.21 = f32[768]{0:T(1024)} reshape(f32[4,192]{1,0:T(4,128)S(1)} %slice.18) | data formatting | bytes 6144 | tf_op jit(solution)/shard_map/reshape | solution.py:539
  (1 shorter events, 0.0 us)
Async XLA Ops:
  9.4 11.4 %copy-start = (bf16[192,1728]{1,0:T(8,128)(2,1)S(1)}, bf16[192,1728]{1,0:T(8,128)(2,1)}, u32[]{:S(2)}) copy-start(bf16[192,1728]{1,0:T(8,128)(2,1)} %cw.1) | copy-start | bytes 1990660
  9.4 11.4 %copy-start.1 = (bf16[768,192]{0,1:T(8,128)(2,1)S(1)}, bf16[768,192]{0,1:T(8,128)(2,1)}, u32[]{:S(2)}) copy-start(bf16[768,192]{0,1:T(8,128)(2,1)} %param.12) | copy-start | bytes 884740
  9.4 11.4 %copy-start.2 = (bf16[192,768]{1,0:T(8,128)(2,1)S(1)}, bf16[192,768]{1,0:T(8,128)(2,1)}, u32[]{:S(2)}) copy-start(bf16[192,768]{1,0:T(8,128)(2,1)} %pw.1) | copy-start | bytes 884740

commit v3 on v1

v3 whole, which is shorter than its diff:
```python
import functools

import jax
import jax.numpy as jnp
from jax import lax
from jax.experimental import pallas as pl
from jax.experimental.pallas import tpu as pltpu
from jax.sharding import PartitionSpec as P

MIXER_ONE = -2048144789
MIXER_TWO = -1028477387
GOLDEN_STEP = -1640531535
KEEP_LEVEL = 819
KEEP_SCALE = 1024.0 / 819.0
ROOT = 0.7978845608028654
CUBIC = 0.044715
MESH = pl.DeviceIdType.MESH
FLOWS = 3
BF = jnp.bfloat16
F32 = jnp.float32


def shifted(number, places):
    return lax.shift_right_logical(number, jnp.int32(places) if number.ndim == 0 else jnp.full_like(number, places))


def scramble(number):
    number = number ^ shifted(number, 16)
    number = number * jnp.int32(MIXER_ONE)
    number = number ^ shifted(number, 13)
    number = number * jnp.int32(MIXER_TWO)
    return number ^ shifted(number, 16)


def gelu_both(x):
    square = x * x
    t = jnp.tanh(ROOT * (x + CUBIC * (square * x)))
    cdf = 0.5 * (1.0 + t)
    slope = cdf + (0.5 * ROOT) * x * (1.0 - t * t) * (1.0 + (3.0 * CUBIC) * square)
    return x * cdf, slope


def gelu_only(x):
    t = jnp.tanh(ROOT * (x + CUBIC * (x * x * x)))
    return x * (0.5 * (1.0 + t))


def dot(left, right, dims):
    return lax.dot_general(left, right, (dims, ((), ())), preferred_element_type=F32)


NN = ((1,), (0,))
NT = ((1,), (1,))
TN = ((0,), (0,))


def halo_start(xt, top, west, corner, edge, send, recv):
    n_lat = lax.axis_size("lat")
    n_lon = lax.axis_size("lon")
    pipe = lax.axis_index("pipe")
    lat = lax.axis_index("lat")
    lon = lax.axis_index("lon")
    last = xt.shape[0] - 1
    width = xt.shape[2]
    away = n_lon // 2
    is_first = lat == 0
    north = jnp.where(is_first, 0, lat - 1)
    turn = jnp.where(is_first, away, 0)
    has_south = lat < n_lat - 1
    sources = [
        (pipe, lat, (lon + n_lon - 1) % n_lon),
        (pipe, north, (lon + n_lon - turn) % n_lon),
        (pipe, north, (lon + n_lon - turn - 1 + n_lon) % n_lon),
    ]
    barrier = pltpu.get_barrier_semaphore()
    for peer in sources:
        pl.semaphore_signal(barrier, inc=1, device_id=peer, device_id_type=MESH)
    sends = 1 + jnp.where(has_south, 2, 0) + jnp.where(is_first, 2, 0)

    def copy(src, dst, i, j, peer):
        return pltpu.make_async_remote_copy(
            src_ref=src,
            dst_ref=dst,
            send_sem=send.at[i],
            recv_sem=recv.at[j],
            device_id=peer,
            device_id_type=MESH,
        )

    right = pl.ds(width - 128, 128)

    def pair(row, i, lat_to, lon_to):
        return [
            copy(xt.at[row], top, i, 0, (pipe, lat_to, lon_to % n_lon)),
            copy(xt.at[row, :, right], corner, i + 1, 1, (pipe, lat_to, (lon_to + 1) % n_lon)),
        ]

    south = pair(last, 0, jnp.where(has_south, lat + 1, lat), lon)
    pole = pair(0, 2, lat, lon + away)
    pl.semaphore_wait(barrier, sends)

    @pl.when(has_south)
    def _():
        for item in south:
            item.start()

    @pl.when(is_first)
    def _():
        for item in pole:
            item.start()

    row_id = lax.broadcasted_iota(jnp.int32, (128, 128), 0)
    col_id = lax.broadcasted_iota(jnp.int32, (128, 128), 1)
    total = None
    for q in range(last + 1):
        pick = jnp.where((row_id == 127) & (col_id == q), 1.0, 0.0).astype(BF)
        term = dot(xt[q, :, width - 128 :], pick, NN)
        total = term if total is None else total + term
    edge[...] = total.astype(BF)
    east = copy(edge, west, 4, 2, (pipe, lat, (lon + 1) % n_lon))
    east.start()
    def finish():
        for item in pole:
            item.wait_recv()
        east.wait()

        @pl.when(has_south)
        def _():
            for item in south:
                item.wait_send()

        @pl.when(is_first)
        def _():
            for item in pole:
                item.wait_send()

    return finish


def compute_kernel(
    rows,
    cols,
    total_rows,
    scale,
    key_ref,
    xt,
    cw,
    ew,
    pw,
    bias_ref,
    cot,
    field_out,
    payload,
    patches,
    enc_s,
    act_s,
    cot_s,
    di_s,
    dp_s,
    top,
    west,
    corner,
    edge_s,
    send,
    recv,
):
    channels, taps = cw.shape
    hidden = ew.shape[1]
    cells = rows * cols
    pad_taps = patches.shape[0]
    is_encoder = lax.axis_index("pipe") == 0
    lon_cols = cols * lax.axis_size("lon")
    row_base = lax.axis_index("lat") * rows
    col_base = lax.axis_index("lon") * cols

    halo_finish = halo_start(xt, top, west, corner, edge_s, send, recv)

    def selector(first, count):
        shape = (2 * cols, count * cols)
        source = lax.broadcasted_iota(jnp.int32, shape, 0)
        target = lax.broadcasted_iota(jnp.int32, shape, 1)
        tap = target // cols
        wanted = 2 * (target - tap * cols) + tap + first - 1
        return jnp.where(source == wanted, 1.0, 0.0).astype(BF)

    def put(q, b, part):
        places = [(1, q // 2)] if q % 2 else [(a, q // 2 - a // 2) for a in (0, 2)]
        for a, r in places:
            if 0 <= r < rows:
                start = (3 * a + b) * channels
                patches[start : start + channels, r * cols : (r + 1) * cols] = part

    def put_pair(q, line):
        split = dot(line, pair, NN).astype(BF)
        put(q, 1, split[:, :cols])
        put(q, 2, split[:, cols:])

    pair = selector(1, 2)
    for q in range(1, 2 * rows + 1):
        put_pair(q, xt[q - 1])
    edge_row = lax.broadcasted_iota(jnp.int32, (128, cols), 0)
    edge_col = lax.broadcasted_iota(jnp.int32, (128, cols), 1)
    single = selector(0, 1)
    halo_finish()
    put_pair(0, top[...])
    for q in range(2 * rows + 1):
        line = top[...] if q == 0 else xt[q - 1]
        lane = 127 if q == 0 else q - 1
        edge = corner[...] if q == 0 else west[...]
        pick = jnp.where((edge_row == lane) & (edge_col == 0), 1.0, 0.0).astype(BF)
        put(q, 0, (dot(line, single, NN) + dot(edge, pick, NN)).astype(BF))
    patches[taps:, :] = jnp.zeros((pad_taps - taps, cells), BF)

    lanes = lax.broadcasted_iota(jnp.int32, (channels, 128), 1)
    salt = scramble(key_ref[0] + scramble(key_ref[1]))
    step = 2 * cols
    sums = [0.0, 0.0, 0.0]
    for j in range(cells // step):
        here = slice(j * step, (j + 1) * step)
        lane = lax.broadcasted_iota(jnp.int32, (1, step), 1)
        local_row = lane // cols
        cell = (row_base + 2 * j + local_row) * lon_cols + col_base + lane - local_row * cols
        hashed = scramble(cell * jnp.int32(GOLDEN_STEP) + salt)
        bucket = jnp.bitwise_and(shifted(hashed, 8), jnp.int32(1023))
        keep = jnp.where(bucket < KEEP_LEVEL, F32(KEEP_SCALE), F32(0.0))
        pre = dot(cw[...], patches[:taps, here], NN) + bias_ref[:channels]
        value, pre_slope = gelu_both(pre)
        encoded = (value * keep).astype(BF)
        inner = dot(ew[...], encoded, TN) + bias_ref[channels : channels + hidden]
        activated, slope = gelu_both(inner)
        activated = activated.astype(BF)
        scaled = jnp.concatenate([cot[2 * j], cot[2 * j + 1]], axis=1).astype(F32) * scale
        cot_half = scaled.astype(BF)
        d_inner = dot(pw[...], cot_half, TN) * slope
        d_half = d_inner.astype(BF)

        def encoder_part(sums=sums):
            field_out[2 * j] = encoded[:, :cols]
            field_out[2 * j + 1] = encoded[:, cols:]
            d_encoded = (scaled + dot(ew[...], d_half, NN)).astype(BF)
            d_pre = d_encoded.astype(F32) * keep * pre_slope
            dp_s[:, here] = d_pre.astype(BF)
            act_s[0:channels, j * 128 : j * 128 + 128] = jnp.sum(d_pre, axis=1, keepdims=True) + jnp.zeros(
                (channels, 128), F32
            )

        def processor_part():
            processed = (encoded.astype(F32) + dot(pw[...], activated, NN) + bias_ref[channels + hidden :]).astype(BF)
            field_out[2 * j] = processed[:, :cols]
            field_out[2 * j + 1] = processed[:, cols:]
            enc_s[:, here] = encoded
            cot_s[:, here] = cot_half
            di_s[:hidden, here] = activated
            di_s[hidden:, here] = d_half
            bias = jnp.where(lanes == 0, jnp.sum(scaled, axis=1, keepdims=True), 0.0)
            total = jnp.sum(d_inner, axis=1, keepdims=True)
            for k in range(hidden // channels):
                bias = jnp.where(lanes == k + 1, total[k * channels : (k + 1) * channels], bias)
            act_s[0:channels, j * 128 : j * 128 + 128] = bias

        pl.when(is_encoder)(encoder_part)
        pl.when(jnp.logical_not(is_encoder))(processor_part)

    def bias_total():
        total = act_s[:, 0:128]
        for j in range(1, cells // step):
            total = total + act_s[:, j * 128 : j * 128 + 128]
        return total

    blocks = pad_taps // 128

    @pl.when(is_encoder)
    def _():
        for k in range(blocks):
            block = dot(dp_s[...], patches[k * 128 : (k + 1) * 128, :], NT)
            if k == blocks - 1:
                block = jnp.where(lanes == taps - k * 128, bias_total(), block)
            payload[k * channels : (k + 1) * channels, :] = block.astype(BF)

    @pl.when(jnp.logical_not(is_encoder))
    def _():
        per = hidden // 128
        for k in range(per):
            block = dot(cot_s[...], di_s[k * 128 : (k + 1) * 128, :], NT)
            payload[k * channels : (k + 1) * channels, :] = block.astype(BF)
        for k in range(per):
            block = dot(enc_s[...], di_s[hidden + k * 128 : hidden + (k + 1) * 128, :], NT)
            payload[(per + k) * channels : (per + k + 1) * channels, :] = block.astype(BF)
        payload[2 * per * channels : (2 * per + 1) * channels, :] = bias_total().astype(BF)
        rest = (2 * per + 1) * channels
        payload[rest : blocks * channels, :] = jnp.zeros((blocks * channels - rest, 128), BF)

    payload[blocks * channels :, :] = jnp.zeros((total_rows - blocks * channels, 128), BF)


def finish_kernel(taps, hidden, gathered, conv, project, expand, conv_bias, project_bias, expand_bias):
    channels = conv.shape[0]
    blocks = -(-(taps + 1) // 128)
    per = hidden // 128
    for k in range(blocks):
        width = min(128, taps - 128 * k)
        block = gathered[0, k * channels : (k + 1) * channels, :]
        conv[:, 128 * k : 128 * k + width] = block[:, :width].astype(F32)
        if k == blocks - 1:
            pick = lax.broadcasted_iota(jnp.int32, (8, 128), 1) == taps - 128 * k
            conv_bias[...] = dot(jnp.where(pick, 1.0, 0.0).astype(BF), block, NT)[:1]
    for k in range(per):
        here = slice(128 * k, 128 * k + 128)
        project[:, here] = gathered[1, k * channels : (k + 1) * channels, :].astype(F32)
        expand[:, here] = gathered[1, (per + k) * channels : (per + k + 1) * channels, :].astype(F32)
    block = gathered[1, 2 * per * channels : (2 * per + 1) * channels, :]
    pick = lax.broadcasted_iota(jnp.int32, (8, 128), 1) == lax.broadcasted_iota(jnp.int32, (8, 128), 0)
    lines = dot(jnp.where(pick, 1.0, 0.0).astype(BF), block, NT)
    project_bias[...] = lines[:1]
    for k in range(hidden // channels):
        expand_bias[:, k * channels : (k + 1) * channels] = lines[k + 1 : k + 2]


def reduce_kernel(n_x, n_z, flows, payload, out, buf1, s1, buf2, s2, buf3, send, recv):
    pipe = lax.axis_index("pipe")
    lat = lax.axis_index("lat")
    z = lax.axis_index("lon")
    x = lat // 2
    core = lat % 2
    twin = (pipe, 2 * x + 1 - core, z)

    def z_peer(d):
        return (pipe, lat, (z + d) % n_z)

    def xp_peer(dx, dp):
        return ((pipe + dp) % 2, 2 * ((x + dx) % n_x) + core, z)

    others = [(dx, dp) for dp in range(2) for dx in range(n_x) if dx or dp]
    peers = [twin] + [z_peer(d) for d in range(1, n_z)] + [xp_peer(*o) for o in others]
    barrier = pltpu.get_barrier_semaphore()
    for peer in peers:
        pl.semaphore_signal(barrier, inc=1, device_id=peer, device_id_type=MESH)
    pl.semaphore_wait(barrier, len(peers))

    count = [0]
    started = []

    def push(src, dst, peer):
        i = count[0]
        count[0] += 1
        copy = pltpu.make_async_remote_copy(
            src_ref=src,
            dst_ref=dst,
            send_sem=send.at[i],
            recv_sem=recv.at[i],
            device_id=peer,
            device_id_type=MESH,
        )
        copy.start()
        started.append(copy)
        return copy

    def at(start, size):
        return pl.ds(pl.multiple_of(start, 16), size)

    halves = [size // 2 for _, size in flows]
    parts = [half // n_x for half in halves]
    owns = [part // n_z for part in parts]
    ids = range(len(flows))

    firsts = []
    for f in ids:
        start = flows[f][0]
        half = halves[f]
        source = payload.at[at(start + (1 - core) * half, half)]
        firsts.append(push(source, buf1.at[f, pl.ds(0, half)], twin))

    seconds = []
    for f in ids:
        half, part = halves[f], parts[f]
        firsts[f].wait_recv()
        kept = payload[at(flows[f][0] + core * half, half), :]
        s1[f, :half] = (kept.astype(F32) + buf1[f, :half].astype(F32)).astype(BF)
        seconds.append(
            [
                push(
                    s1.at[f, at(((x + d) % n_x) * part, part)],
                    buf2.at[f, d - 1, pl.ds(0, part)],
                    xp_peer(d, 0),
                )
                for d in range(1, n_x)
            ]
        )

    thirds = []
    for f in ids:
        part, own = parts[f], owns[f]
        total = s1[f, at(x * part, part), :].astype(F32)
        for d in range(1, n_x):
            seconds[f][d - 1].wait_recv()
            total = total + buf2[f, d - 1, :part].astype(F32)
        s2[f, :part] = total.astype(BF)
        thirds.append(
            [
                push(
                    s2.at[f, at(((z + d) % n_z) * own, own)],
                    buf3.at[f, d - 1, pl.ds(0, own)],
                    z_peer(d),
                )
                for d in range(1, n_z)
            ]
        )

    fourths = []
    for f in ids:
        part, own = parts[f], owns[f]
        total = s2[f, at(z * own, own), :].astype(F32)
        for d in range(1, n_z):
            thirds[f][d - 1].wait_recv()
            total = total + buf3[f, d - 1, :own].astype(F32)
        place = at(flows[f][0] + core * halves[f] + x * part + z * own, own)
        mine = out.at[pipe, place]
        mine[...] = total.astype(BF)
        fourths.append([push(mine, mine, z_peer(d)) for d in range(1, n_z)])

    fifths = []
    final = []
    for f in ids:
        for copy in fourths[f]:
            copy.wait_recv()
        column = out.at[pipe, at(flows[f][0] + core * halves[f] + x * parts[f], parts[f])]
        fifths.append([push(column, column, xp_peer(*o)) for o in others])
        final.append(push(column, column, twin))
    for f in ids:
        for (dx, dp), copy in zip(others, fifths[f]):
            copy.wait_recv()
            start = flows[f][0] + core * halves[f] + ((x - dx + n_x) % n_x) * parts[f]
            block = out.at[(pipe + dp) % 2, at(start, parts[f])]
            final.append(push(block, block, twin))
    for copy in final:
        copy.wait_recv()
    for copy in started:
        copy.wait_send()


def per_device(
    field,
    conv_weight,
    conv_bias,
    expand_weight,
    expand_bias,
    project_weight,
    project_bias,
    out_cotangent,
    dropout_key,
):
    channels, row_count, col_count = field.shape
    hidden = expand_weight.shape[0]
    taps = conv_weight.shape[1]
    rows = row_count // 2
    cols = col_count // 2
    cells = rows * cols
    n_lat = lax.axis_size("lat")
    n_lon = lax.axis_size("lon")
    scale = float(cells * n_lat * n_lon) ** (-0.5)

    pad_taps = -(-(taps + 1) // 128) * 128
    blocks = pad_taps // 128
    unit = 16 * n_lat * n_lon
    total_rows = -(-(blocks * channels) // unit) * unit
    vmem = pl.BlockSpec(memory_space=pltpu.VMEM)
    smem = pl.BlockSpec(memory_space=pltpu.SMEM)
    turned = jnp.transpose(field, (1, 0, 2))
    field_out, payload = pl.pallas_call(
        functools.partial(compute_kernel, rows, cols, total_rows, scale),
        out_shape=(
            jax.ShapeDtypeStruct((rows, channels, cols), BF),
            jax.ShapeDtypeStruct((total_rows, 128), BF),
        ),
        in_specs=[smem] + [vmem] * 6,
        out_specs=(vmem, vmem),
        scratch_shapes=[
            pltpu.VMEM((pad_taps, cells), BF),
            pltpu.VMEM((channels, cells), BF),
            pltpu.VMEM((channels, cells // (2 * cols) * 128), F32),
            pltpu.VMEM((channels, cells), BF),
            pltpu.VMEM((2 * hidden, cells), BF),
            pltpu.VMEM((channels, cells), BF),
            pltpu.VMEM((channels, col_count), BF),
            pltpu.VMEM((channels, 128), BF),
            pltpu.VMEM((channels, 128), BF),
            pltpu.VMEM((channels, 128), BF),
            pltpu.SemaphoreType.DMA((5,)),
            pltpu.SemaphoreType.DMA((3,)),
        ],
        compiler_params=pltpu.CompilerParams(
            collective_id=1, has_side_effects=True, vmem_limit_bytes=40 * 1024 * 1024
        ),
        name="segment",
    )(
        dropout_key,
        turned,
        conv_weight,
        expand_weight.T,
        project_weight,
        jnp.concatenate([conv_bias, expand_bias, project_bias])[:, None],
        jnp.transpose(out_cotangent, (1, 0, 2)),
    )

    n_x = n_lat // 2
    units = total_rows // unit
    count = min(FLOWS, units)
    sizes = [(units // count + (1 if f < units % count else 0)) * unit for f in range(count)]
    flows = [(sum(sizes[:f]), sizes[f]) for f in range(count)]
    half = sizes[0] // 2
    part = half // n_x
    own = part // n_lon
    copies = count * (1 + (n_x - 1) + 2 * (n_lon - 1) + 2 * (2 * n_x - 1) + 1)
    gathered = pl.pallas_call(
        functools.partial(reduce_kernel, n_x, n_lon, flows),
        out_shape=jax.ShapeDtypeStruct((2, total_rows, 128), BF),
        in_specs=[vmem],
        out_specs=vmem,
        scratch_shapes=[
            pltpu.VMEM((count, half, 128), BF),
            pltpu.VMEM((count, half, 128), BF),
            pltpu.VMEM((count, n_x - 1, part, 128), BF),
            pltpu.VMEM((count, part, 128), BF),
            pltpu.VMEM((count, n_lon - 1, own, 128), BF),
            pltpu.SemaphoreType.DMA((copies,)),
            pltpu.SemaphoreType.DMA((copies,)),
        ],
        compiler_params=pltpu.CompilerParams(
            collective_id=0, has_side_effects=True, vmem_limit_bytes=40 * 1024 * 1024
        ),
        name="gradient_sum",
    )(payload)

    wide = jax.ShapeDtypeStruct((channels, hidden), F32)
    short = jax.ShapeDtypeStruct((1, channels), F32)
    longer = jax.ShapeDtypeStruct((1, hidden), F32)
    conv_grad, project_grad, expand_turned, conv_row, project_row, expand_row = pl.pallas_call(
        functools.partial(finish_kernel, taps, hidden),
        out_shape=(jax.ShapeDtypeStruct((channels, taps), F32), wide, wide, short, short, longer),
        in_specs=[vmem],
        out_specs=(vmem,) * 6,
        compiler_params=pltpu.CompilerParams(vmem_limit_bytes=32 * 1024 * 1024),
        name="widen",
    )(gathered)
    expand_grad = expand_turned.T
    conv_bias_grad = conv_row[0]
    project_bias_grad = project_row[0]
    expand_bias_grad = expand_row[0]
    section_fields = jnp.transpose(field_out, (1, 0, 2))[None]
    return (
        section_fields,
        conv_grad,
        conv_bias_grad,
        expand_grad,
        expand_bias_grad,
        project_grad,
        project_bias_grad,
    )


def solution(mesh):
    placed = (P(None, "lat", "lon"), P(), P(), P(), P(), P(), P(), P(None, "lat", "lon"), P())
    return jax.shard_map(
        per_device,
        mesh=mesh,
        in_specs=placed,
        out_specs=(P("pipe", None, "lat", "lon"), P(), P(), P(), P(), P(), P()),
        check_vma=False,
    )
```

time: 70.4 us -> 54.1 us (0.77)
  local copies, waits for them, and re-layouts: 13.7 us -> 5.1 us
  starting transfers between devices: 7.95 us -> 0 us
  Pallas kernels: 39.6 us -> 47.5 us
  waiting for transfers between devices: 4.72 us -> 0 us
  between operations: 2.82 us -> 0.73 us
  other arithmetic: 1.37 us -> 0.61 us
    pallas_call x1, Pallas kernels: 9.41 us -> 20.7 us  [per_device(): pl.pallas_call(functools.partial(compute_kernel, rows, cols, total_rows,...]
    ppermute x3 -> x0, starting transfers between devices: 7.95 us -> none  [the longest x2 4.95 us: passed_along(): return lax.ppermute(value, axis, pairs)]
    unnamed x27 -> x11, local copies, waits for them, and re-layouts: 8.94 us -> 4.11 us
    ppermute x3 -> x0, waiting for transfers between devices: 4.72 us -> none  [the longest x2 4.72 us: passed_along(): return lax.ppermute(value, axis, pairs)]
    pallas_call x1 -> x2, Pallas kernels: 30.2 us -> 26.8 us  [the longest x1 25.1 us: per_device(): pl.pallas_call(functools.partial(reduce_kernel, n_x, n_lon, flows), out_s...]
    slice x9 -> x0, local copies, waits for them, and re-layouts: 2.62 us -> none  [the longest x1 0.92 us: per_device(): conv_bias_grad = wide[:, taps]]
    select_n x1 -> x0, other arithmetic: 0.91 us -> none  [per_device(): top = jnp.where(lax.axis_index('lat') == 0, mirrored, from_above)]
    concatenate x0 -> x1, local copies, waits for them, and re-layouts: none -> 0.79 us  [per_device(): jnp.concatenate([conv_bias, expand_bias, project_bias])[:, None]]
  transfers between devices with their start and end apart: 3 -> 0, of which waited for: 2 -> 0; matrix products, arithmetic and copies ran while one was open for 5% -> 0% of each run, Pallas kernels for 0% -> 0%
where the time goes in v3:
time: 54.1 us; the launch traced here: 53.9 us
  Pallas kernels  47.5 us (88%)
  local copies, waits for them, and re-layouts  5.1 us (9%)
  between operations  0.73 us (1%)
  other arithmetic  0.61 us (1%)
    pallas_call x1, Pallas kernels, per_device(): pl.pallas_call(functools.partial(reduce_kernel, n_x, n_lon, flows), out_s...  25.1 us
    pallas_call x1, Pallas kernels, per_device(): pl.pallas_call(functools.partial(compute_kernel, rows, cols, total_rows,...  20.7 us
    unnamed x11, local copies, waits for them, and re-layouts  4.11 us
    pallas_call x1, Pallas kernels, per_device(): pl.pallas_call(functools.partial(finish_kernel, taps, hidden), out_shape=...  1.66 us

profile of v3, /device:TPU:0, one launch (start us, length us, event | category | flops | bytes accessed | tf_op | source)
XLA Modules:
  0.0 53.9 jit_solution(4104704568928893711)
XLA Ops:
  0.6 0.8 %concatenate.3 = f32[1152]{0:T(1024)S(1)} concatenate(f32[192]{0:T(256)} %param.11, f32[768]{0:T(1024)} %param.13, f32[192]{0:T(256)} %param.15), dimensions={0} | concatenate | bytes 9216 | tf_op jit(solution)/shard_map/concatenate | solution.py:501
  1.4 1.0 %copy.26 = bf16[192,8,128]{2,0,1:T(8,128)(2,1)S(1)} copy(bf16[192,8,128]{2,1,0:T(8,128)(2,1)} %param.16) | data formatting | bytes 786432 | tf_op args[7]
  2.5 0.2 broadcast_in_dim.8.bias_ref
  2.7 0.0 copy-start
  2.7 0.0 copy-start.1
  2.7 0.0 copy-start.2
  2.7 0.0 copy-start.3
  2.7 2.0 %copy.25 = bf16[192,16,256]{2,0,1:T(8,128)(2,1)S(1)} copy(bf16[192,16,256]{2,1,0:T(8,128)(2,1)} %param.9) | data formatting | bytes 3145728 | tf_op args[0]
  4.8 0.0 copy-done
  4.8 0.0 copy-done.1
  4.8 0.0 copy-done.2
  4.8 0.0 copy-done.3
  4.8 20.7 %segment.1 = (bf16[8,192,128]{2,1,0:T(8,128)(2,1)S(1)}, bf16[2816,128]{1,0:T(8,128)(2,1)S(1)}) custom-call(s32[2]{0:T(128)S(1)} %copy-done.3, bf16[16,192,256]{2,1,0:T(8,128)(2,1)S(1)} %bitcast.13, bf16[192,1728]{1,0:T(8,128)(2,1)S(1)} %copy-done, bf16[192,768]{1,0:T(8,128)(2,1)S(1)} %bitcast.16, bf16[192,768]{1,0:T(8,128)(2,1)S(1)} %copy-done.2, ...), custom_call_target="tpu_custom_call" | custom-call | tf_op jit(solution)/shard_map/segment/pallas_call | solution.py:469
  25.5 1.0 %copy.22 = bf16[1,192,8,128]{3,2,1,0:T(8,128)(2,1)} copy(bf16[1,192,8,128]{3,1,2,0:T(8,128)(2,1)S(1)} %bitcast.15) | data formatting | bytes 786432
  26.5 25.1 %gradient_sum.1.gathered = bf16[2,2816,128]{2,1,0:T(8,128)(2,1)S(1)} custom-call(bf16[2816,128]{1,0:T(8,128)(2,1)S(1)} %get-tuple-element.16.payload), custom_call_target="tpu_custom_call" | custom-call | tf_op jit(solution)/shard_map/gradient_sum/pallas_call | solution.py:514
  51.7 1.7 %widen.1 = (f32[192,1728]{1,0:T(8,128)}, f32[192,768]{1,0:T(8,128)}, f32[192,768]{1,0:T(8,128)}, f32[1,192]{1,0:T(1,128)}, f32[1,192]{1,0:T(1,128)}, /*index=5*/f32[1,768]{1,0:T(1,128)S(1)}) custom-call(bf16[2,2816,128]{2,1,0:T(8,128)(2,1)S(1)} %gradient_sum.1.gathered), custom_call_target="tpu_custom_call" | custom-call | tf_op jit(solution)/shard_map/widen/pallas_call | solution.py:537
  53.3 0.6 %reduce = f32[768]{0:T(1024)} reduce(f32[1,768]{1,0:T(1,128)S(1)} %get-tuple-element.20, f32[]{:T(128)} %constant), dimensions={0}, to_apply=%get-tuple-element.20.reduce_sub_computation | reduce | bytes 6148 | tf_op jit(solution)/shard_map/widen/pallas_call | solution.py:537
Async XLA Ops:
  2.7 2.1 %copy-start = (bf16[192,1728]{1,0:T(8,128)(2,1)S(1)}, bf16[192,1728]{1,0:T(8,128)(2,1)}, u32[]{:S(2)}) copy-start(bf16[192,1728]{1,0:T(8,128)(2,1)} %cw.1) | copy-start | bytes 1990660
  2.7 2.1 %copy-start.1 = (bf16[768,192]{0,1:T(8,128)(2,1)S(1)}, bf16[768,192]{0,1:T(8,128)(2,1)}, u32[]{:S(2)}) copy-start(bf16[768,192]{0,1:T(8,128)(2,1)} %param.12) | copy-start | bytes 884740
  2.7 2.1 %copy-start.2 = (bf16[192,768]{1,0:T(8,128)(2,1)S(1)}, bf16[192,768]{1,0:T(8,128)(2,1)}, u32[]{:S(2)}) copy-start(bf16[192,768]{1,0:T(8,128)(2,1)} %pw.1) | copy-start | bytes 884740
  2.7 2.1 %copy-start.3 = (s32[2]{0:T(128)S(1)}, s32[2]{0:T(128)}, u32[]{:S(2)}) copy-start(s32[2]{0:T(128)} %key_ref.1) | copy-start | bytes 28

commit v4 on v3

--- a/solution.py
+++ b/solution.py
@@ -15,7 +15,7 @@
 ROOT = 0.7978845608028654
 CUBIC = 0.044715
 MESH = pl.DeviceIdType.MESH
-FLOWS = 3
+FLOWS = 4
 BF = jnp.bfloat16
 F32 = jnp.float32
 
@@ -54,7 +54,7 @@
 TN = ((0,), (0,))
 
 
-def halo_start(xt, top, west, corner, edge, send, recv):
+def halo_start(peers, xt, top, west, corner, edge, send, recv):
     n_lat = lax.axis_size("lat")
     n_lon = lax.axis_size("lon")
     pipe = lax.axis_index("pipe")
@@ -73,9 +73,9 @@
         (pipe, north, (lon + n_lon - turn - 1 + n_lon) % n_lon),
     ]
     barrier = pltpu.get_barrier_semaphore()
-    for peer in sources:
+    for peer in sources + peers:
         pl.semaphore_signal(barrier, inc=1, device_id=peer, device_id_type=MESH)
-    sends = 1 + jnp.where(has_south, 2, 0) + jnp.where(is_first, 2, 0)
+    sends = len(peers) + 1 + jnp.where(has_south, 2, 0) + jnp.where(is_first, 2, 0)
 
     def copy(src, dst, i, j, peer):
         return pltpu.make_async_remote_copy(
@@ -137,11 +137,135 @@
     return finish
 
 
+def reduce_parts(flows, payload, out, buf1, s1, buf2, s2, buf3, send, recv):
+    n_x = lax.axis_size("lat") // 2
+    n_z = lax.axis_size("lon")
+    pipe = lax.axis_index("pipe")
+    lat = lax.axis_index("lat")
+    z = lax.axis_index("lon")
+    x = lat // 2
+    core = lat % 2
+    twin = (pipe, 2 * x + 1 - core, z)
+
+    def z_peer(d):
+        return (pipe, lat, (z + d) % n_z)
+
+    def xp_peer(dx, dp):
+        return ((pipe + dp) % 2, 2 * ((x + dx) % n_x) + core, z)
+
+    others = [(dx, dp) for dp in range(2) for dx in range(n_x) if dx or dp]
+    peers = [twin] + [z_peer(d) for d in range(1, n_z)] + [xp_peer(*o) for o in others]
+    count = [0]
+    started = []
+
+    def push(src, dst, peer):
+        i = count[0]
+        count[0] += 1
+        copy = pltpu.make_async_remote_copy(
+            src_ref=src,
+            dst_ref=dst,
+            send_sem=send.at[i],
+            recv_sem=recv.at[i],
+            device_id=peer,
+            device_id_type=MESH,
+        )
+        copy.start()
+        started.append(copy)
+        return copy
+
+    def at(start, size):
+        return pl.ds(pl.multiple_of(start, 16), size)
+
+    halves = [size // 2 for _, size in flows]
+    parts = [half // n_x for half in halves]
+    owns = [part // n_z for part in parts]
+    ids = range(len(flows))
+
+    firsts = []
+
+    def begin(f):
+        start = flows[f][0]
+        half = halves[f]
+        source = payload.at[at(start + (1 - core) * half, half)]
+        firsts.append(push(source, buf1.at[f, pl.ds(0, half)], twin))
+
+    def complete():
+        seconds = []
+        for f in ids:
+            half, part = halves[f], parts[f]
+            firsts[f].wait_recv()
+            kept = payload[at(flows[f][0] + core * half, half), :]
+            s1[f, :half] = (kept.astype(F32) + buf1[f, :half].astype(F32)).astype(BF)
+            seconds.append(
+                [
+                    push(
+                        s1.at[f, at(((x + d) % n_x) * part, part)],
+                        buf2.at[f, d - 1, pl.ds(0, part)],
+                        xp_peer(d, 0),
+                    )
+                    for d in range(1, n_x)
+                ]
+            )
+
+        thirds = []
+        for f in ids:
+            part, own = parts[f], owns[f]
+            total = s1[f, at(x * part, part), :].astype(F32)
+            for d in range(1, n_x):
+                seconds[f][d - 1].wait_recv()
+                total = total + buf2[f, d - 1, :part].astype(F32)
+            s2[f, :part] = total.astype(BF)
+            thirds.append(
+                [
+                    push(
+                        s2.at[f, at(((z + d) % n_z) * own, own)],
+                        buf3.at[f, d - 1, pl.ds(0, own)],
+                        z_peer(d),
+                    )
+                    for d in range(1, n_z)
+                ]
+            )
+
+        fourths = []
+        for f in ids:
+            part, own = parts[f], owns[f]
+            total = s2[f, at(z * own, own), :].astype(F32)
+            for d in range(1, n_z):
+                thirds[f][d - 1].wait_recv()
+                total = total + buf3[f, d - 1, :own].astype(F32)
+            place = at(flows[f][0] + core * halves[f] + x * part + z * own, own)
+            mine = out.at[pipe, place]
+            mine[...] = total.astype(BF)
+            fourths.append([push(mine, mine, z_peer(d)) for d in range(1, n_z)])
+
+        fifths = []
+        final = []
+        for f in ids:
+            for copy in fourths[f]:
+                copy.wait_recv()
+            column = out.at[pipe, at(flows[f][0] + core * halves[f] + x * parts[f], parts[f])]
+            fifths.append([push(column, column, xp_peer(*o)) for o in others])
+            final.append(push(column, column, twin))
+        for f in ids:
+            for (dx, dp), copy in zip(others, fifths[f]):
+                copy.wait_recv()
+                start = flows[f][0] + core * halves[f] + ((x - dx + n_x) % n_x) * parts[f]
+                block = out.at[(pipe + dp) % 2, at(start, parts[f])]
+                final.append(push(block, block, twin))
+        for copy in final:
+            copy.wait_recv()
+        for copy in started:
+            copy.wait_send()
+
+    return peers, begin, complete
+
+
 def compute_kernel(
     rows,
     cols,
     total_rows,
     scale,
+    flows,
     key_ref,
     xt,
     cw,
@@ -150,7 +274,7 @@
     bias_ref,
     cot,
     field_out,
-    payload,
+    out,
     patches,
     enc_s,
     act_s,
@@ -163,6 +287,14 @@
     edge_s,
     send,
     recv,
+    payload,
+    buf1,
+    s1,
+    buf2,
+    s2,
+    buf3,
+    sum_send,
+    sum_recv,
 ):
     channels, taps = cw.shape
     hidden = ew.shape[1]
@@ -173,7 +305,10 @@
     row_base = lax.axis_index("lat") * rows
     col_base = lax.axis_index("lon") * cols
 
-    halo_finish = halo_start(xt, top, west, corner, edge_s, send, recv)
+    peers, begin, complete = reduce_parts(
+        flows, payload, out, buf1, s1, buf2, s2, buf3, sum_send, sum_recv
+    )
+    halo_finish = halo_start(peers, xt, top, west, corner, edge_s, send, recv)
 
     def selector(first, count):
         shape = (2 * cols, count * cols)
@@ -269,28 +404,45 @@
 
     blocks = pad_taps // 128
 
-    @pl.when(is_encoder)
-    def _():
-        for k in range(blocks):
-            block = dot(dp_s[...], patches[k * 128 : (k + 1) * 128, :], NT)
-            if k == blocks - 1:
-                block = jnp.where(lanes == taps - k * 128, bias_total(), block)
-            payload[k * channels : (k + 1) * channels, :] = block.astype(BF)
-
-    @pl.when(jnp.logical_not(is_encoder))
-    def _():
-        per = hidden // 128
-        for k in range(per):
-            block = dot(cot_s[...], di_s[k * 128 : (k + 1) * 128, :], NT)
-            payload[k * channels : (k + 1) * channels, :] = block.astype(BF)
-        for k in range(per):
-            block = dot(enc_s[...], di_s[hidden + k * 128 : hidden + (k + 1) * 128, :], NT)
-            payload[(per + k) * channels : (per + k + 1) * channels, :] = block.astype(BF)
-        payload[2 * per * channels : (2 * per + 1) * channels, :] = bias_total().astype(BF)
-        rest = (2 * per + 1) * channels
-        payload[rest : blocks * channels, :] = jnp.zeros((blocks * channels - rest, 128), BF)
+    per = hidden // 128
+
+    def encoder_block(k):
+        here = slice(k * channels, (k + 1) * channels)
+        block = dot(dp_s[...], patches[k * 128 : (k + 1) * 128, :], NT)
+        if k == blocks - 1:
+            block = jnp.where(lanes == taps - k * 128, bias_total(), block)
+        payload[here, :] = block.astype(BF)
+
+    def processor_block(k):
+        here = slice(k * channels, (k + 1) * channels)
+        if k < 2 * per:
+            left = cot_s if k < per else enc_s
+            block = dot(left[...], di_s[k * 128 : (k + 1) * 128, :], NT)
+        elif k == 2 * per:
+            block = bias_total()
+        else:
+            block = jnp.zeros((channels, 128), F32)
+        payload[here, :] = block.astype(BF)
 
     payload[blocks * channels :, :] = jnp.zeros((total_rows - blocks * channels, 128), BF)
+    done = 0
+    for f, (start, size) in enumerate(flows):
+        upto = min(blocks, -(-(start + size) // channels))
+        todo = range(done, upto)
+        done = upto
+
+        @pl.when(is_encoder)
+        def _(todo=todo):
+            for k in todo:
+                encoder_block(k)
+
+        @pl.when(jnp.logical_not(is_encoder))
+        def _(todo=todo):
+            for k in todo:
+                processor_block(k)
+
+        begin(f)
+    complete()
 
 
 def finish_kernel(taps, hidden, gathered, conv, project, expand, conv_bias, project_bias, expand_bias):
@@ -316,128 +468,6 @@
         expand_bias[:, k * channels : (k + 1) * channels] = lines[k + 1 : k + 2]
 
 
-def reduce_kernel(n_x, n_z, flows, payload, out, buf1, s1, buf2, s2, buf3, send, recv):
-    pipe = lax.axis_index("pipe")
-    lat = lax.axis_index("lat")
-    z = lax.axis_index("lon")
-    x = lat // 2
-    core = lat % 2
-    twin = (pipe, 2 * x + 1 - core, z)
-
-    def z_peer(d):
-        return (pipe, lat, (z + d) % n_z)
-
-    def xp_peer(dx, dp):
-        return ((pipe + dp) % 2, 2 * ((x + dx) % n_x) + core, z)
-
-    others = [(dx, dp) for dp in range(2) for dx in range(n_x) if dx or dp]
-    peers = [twin] + [z_peer(d) for d in range(1, n_z)] + [xp_peer(*o) for o in others]
-    barrier = pltpu.get_barrier_semaphore()
-    for peer in peers:
-        pl.semaphore_signal(barrier, inc=1, device_id=peer, device_id_type=MESH)
-    pl.semaphore_wait(barrier, len(peers))
-
-    count = [0]
-    started = []
-
-    def push(src, dst, peer):
-        i = count[0]
-        count[0] += 1
-        copy = pltpu.make_async_remote_copy(
-            src_ref=src,
-            dst_ref=dst,
-            send_sem=send.at[i],
-            recv_sem=recv.at[i],
-            device_id=peer,
-            device_id_type=MESH,
-        )
-        copy.start()
-        started.append(copy)
-        return copy
-
-    def at(start, size):
-        return pl.ds(pl.multiple_of(start, 16), size)
-
-    halves = [size // 2 for _, size in flows]
-    parts = [half // n_x for half in halves]
-    owns = [part // n_z for part in parts]
-    ids = range(len(flows))
-
-    firsts = []
-    for f in ids:
-        start = flows[f][0]
-        half = halves[f]
-        source = payload.at[at(start + (1 - core) * half, half)]
-        firsts.append(push(source, buf1.at[f, pl.ds(0, half)], twin))
-
-    seconds = []
-    for f in ids:
-        half, part = halves[f], parts[f]
-        firsts[f].wait_recv()
-        kept = payload[at(flows[f][0] + core * half, half), :]
-        s1[f, :half] = (kept.astype(F32) + buf1[f, :half].astype(F32)).astype(BF)
-        seconds.append(
-            [
-                push(
-                    s1.at[f, at(((x + d) % n_x) * part, part)],
-                    buf2.at[f, d - 1, pl.ds(0, part)],
-                    xp_peer(d, 0),
-                )
-                for d in range(1, n_x)
-            ]
-        )
-
-    thirds = []
-    for f in ids:
-        part, own = parts[f], owns[f]
-        total = s1[f, at(x * part, part), :].astype(F32)
-        for d in range(1, n_x):
-            seconds[f][d - 1].wait_recv()
-            total = total + buf2[f, d - 1, :part].astype(F32)
-        s2[f, :part] = total.astype(BF)
-        thirds.append(
-            [
-                push(
-                    s2.at[f, at(((z + d) % n_z) * own, own)],
-                    buf3.at[f, d - 1, pl.ds(0, own)],
-                    z_peer(d),
-                )
-                for d in range(1, n_z)
-            ]
-        )
-
-    fourths = []
-    for f in ids:
-        part, own = parts[f], owns[f]
-        total = s2[f, at(z * own, own), :].astype(F32)
-        for d in range(1, n_z):
-            thirds[f][d - 1].wait_recv()
-            total = total + buf3[f, d - 1, :own].astype(F32)
-        place = at(flows[f][0] + core * halves[f] + x * part + z * own, own)
-        mine = out.at[pipe, place]
-        mine[...] = total.astype(BF)
-        fourths.append([push(mine, mine, z_peer(d)) for d in range(1, n_z)])
-
-    fifths = []
-    final = []
-    for f in ids:
-        for copy in fourths[f]:
-            copy.wait_recv()
-        column = out.at[pipe, at(flows[f][0] + core * halves[f] + x * parts[f], parts[f])]
-        fifths.append([push(column, column, xp_peer(*o)) for o in others])
-        final.append(push(column, column, twin))
-    for f in ids:
-        for (dx, dp), copy in zip(others, fifths[f]):
-            copy.wait_recv()
-            start = flows[f][0] + core * halves[f] + ((x - dx + n_x) % n_x) * parts[f]
-            block = out.at[(pipe + dp) % 2, at(start, parts[f])]
-            final.append(push(block, block, twin))
-    for copy in final:
-        copy.wait_recv()
-    for copy in started:
-        copy.wait_send()
-
-
 def per_device(
     field,
     conv_weight,
@@ -465,12 +495,21 @@
     total_rows = -(-(blocks * channels) // unit) * unit
     vmem = pl.BlockSpec(memory_space=pltpu.VMEM)
     smem = pl.BlockSpec(memory_space=pltpu.SMEM)
+    n_x = n_lat // 2
+    units = total_rows // unit
+    count = min(FLOWS, units)
+    sizes = [(units // count + (1 if f < units % count else 0)) * unit for f in range(count)]
+    flows = [(sum(sizes[:f]), sizes[f]) for f in range(count)]
+    half = sizes[0] // 2
+    part = half // n_x
+    own = part // n_lon
+    copies = count * (1 + (n_x - 1) + 2 * (n_lon - 1) + 2 * (2 * n_x - 1) + 1)
     turned = jnp.transpose(field, (1, 0, 2))
-    field_out, payload = pl.pallas_call(
-        functools.partial(compute_kernel, rows, cols, total_rows, scale),
+    field_out, gathered = pl.pallas_call(
+        functools.partial(compute_kernel, rows, cols, total_rows, scale, flows),
         out_shape=(
             jax.ShapeDtypeStruct((rows, channels, cols), BF),
-            jax.ShapeDtypeStruct((total_rows, 128), BF),
+            jax.ShapeDtypeStruct((2, total_rows, 128), BF),
         ),
         in_specs=[smem] + [vmem] * 6,
         out_specs=(vmem, vmem),
@@ -487,6 +526,14 @@
             pltpu.VMEM((channels, 128), BF),
             pltpu.SemaphoreType.DMA((5,)),
             pltpu.SemaphoreType.DMA((3,)),
+            pltpu.VMEM((total_rows, 128), BF),
+            pltpu.VMEM((count, half, 128), BF),
+            pltpu.VMEM((count, half, 128), BF),
+            pltpu.VMEM((count, n_x - 1, part, 128), BF),
+            pltpu.VMEM((count, part, 128), BF),
+            pltpu.VMEM((count, n_lon - 1, own, 128), BF),
+            pltpu.SemaphoreType.DMA((copies,)),
+            pltpu.SemaphoreType.DMA((copies,)),
         ],
         compiler_params=pltpu.CompilerParams(
             collective_id=1, has_side_effects=True, vmem_limit_bytes=40 * 1024 * 1024
@@ -501,35 +548,6 @@
         jnp.concatenate([conv_bias, expand_bias, project_bias])[:, None],
         jnp.transpose(out_cotangent, (1, 0, 2)),
     )
-
-    n_x = n_lat // 2
-    units = total_rows // unit
-    count = min(FLOWS, units)
-    sizes = [(units // count + (1 if f < units % count else 0)) * unit for f in range(count)]
-    flows = [(sum(sizes[:f]), sizes[f]) for f in range(count)]
-    half = sizes[0] // 2
-    part = half // n_x
-    own = part // n_lon
-    copies = count * (1 + (n_x - 1) + 2 * (n_lon - 1) + 2 * (2 * n_x - 1) + 1)
-    gathered = pl.pallas_call(
-        functools.partial(reduce_kernel, n_x, n_lon, flows),
-        out_shape=jax.ShapeDtypeStruct((2, total_rows, 128), BF),
-        in_specs=[vmem],
-        out_specs=vmem,
-        scratch_shapes=[
-            pltpu.VMEM((count, half, 128), BF),
-            pltpu.VMEM((count, half, 128), BF),
-            pltpu.VMEM((count, n_x - 1, part, 128), BF),
-            pltpu.VMEM((count, part, 128), BF),
-            pltpu.VMEM((count, n_lon - 1, own, 128), BF),
-            pltpu.SemaphoreType.DMA((copies,)),
-            pltpu.SemaphoreType.DMA((copies,)),
-        ],
-        compiler_params=pltpu.CompilerParams(
-            collective_id=0, has_side_effects=True, vmem_limit_bytes=40 * 1024 * 1024
-        ),
-        name="gradient_sum",
-    )(payload)
 
     wide = jax.ShapeDtypeStruct((channels, hidden), F32)
     short = jax.ShapeDtypeStruct((1, channels), F32)

time: 54.1 us -> 51.4 us (0.950)
  Pallas kernels: 47.5 us -> 44.8 us
    pallas_call x1 -> x0, Pallas kernels: 25.1 us -> none  [per_device(): pl.pallas_call(functools.partial(reduce_kernel, n_x, n_lon, flows), out_s...]
    pallas_call x1, Pallas kernels: 20.7 us -> 43.1 us  [per_device(): pl.pallas_call(functools.partial(compute_kernel, rows, cols, total_rows,...]
where the time goes in v4:
time: 51.4 us; the launch traced here: 51.2 us
  Pallas kernels  44.8 us (87%)
  local copies, waits for them, and re-layouts  5.1 us (10%)
  between operations  0.72 us (1%)
  other arithmetic  0.61 us (1%)
    pallas_call x1, Pallas kernels, per_device(): pl.pallas_call(functools.partial(compute_kernel, rows, cols, total_rows,...  43.1 us
    unnamed x11, local copies, waits for them, and re-layouts  4.11 us
    pallas_call x1, Pallas kernels, per_device(): pl.pallas_call(functools.partial(finish_kernel, taps, hidden), out_shape=...  1.66 us

profile of v4, /device:TPU:0, one launch (start us, length us, event | category | flops | bytes accessed | tf_op | source)
XLA Modules:
  0.0 51.2 jit_solution(16321541190500084290)
XLA Ops:
  0.6 0.8 %concatenate.3 = f32[1152]{0:T(1024)S(1)} concatenate(f32[192]{0:T(256)} %param.11, f32[768]{0:T(1024)} %param.13, f32[192]{0:T(256)} %param.15), dimensions={0} | concatenate | bytes 9216 | tf_op jit(solution)/shard_map/concatenate | solution.py:548
  1.4 1.0 %copy.26 = bf16[192,8,128]{2,0,1:T(8,128)(2,1)S(1)} copy(bf16[192,8,128]{2,1,0:T(8,128)(2,1)} %param.16) | data formatting | bytes 786432 | tf_op args[7]
  2.5 0.2 broadcast_in_dim.8.bias_ref
  2.7 0.0 copy-start
  2.7 0.0 copy-start.1
  2.7 0.0 copy-start.2
  2.7 0.0 copy-start.3
  2.7 2.0 %copy.25 = bf16[192,16,256]{2,0,1:T(8,128)(2,1)S(1)} copy(bf16[192,16,256]{2,1,0:T(8,128)(2,1)} %param.9) | data formatting | bytes 3145728 | tf_op args[0]
  4.8 0.0 copy-done
  4.8 0.0 copy-done.1
  4.8 0.0 copy-done.2
  4.8 0.0 copy-done.3
  4.8 43.1 %segment.1 = (bf16[8,192,128]{2,1,0:T(8,128)(2,1)S(1)}, bf16[2,2816,128]{2,1,0:T(8,128)(2,1)S(1)}) custom-call(s32[2]{0:T(128)S(1)} %copy-done.3, bf16[16,192,256]{2,1,0:T(8,128)(2,1)S(1)} %bitcast.13, bf16[192,1728]{1,0:T(8,128)(2,1)S(1)} %copy-done, bf16[192,768]{1,0:T(8,128)(2,1)S(1)} %bitcast.16, bf16[192,768]{1,0:T(8,128)(2,1)S(1)} %copy-done.2, ...), custom_call_target="tpu_custom_call" | custom-call | tf_op jit(solution)/shard_map/segment/pallas_call | solution.py:508
  47.9 1.0 %copy.22 = bf16[1,192,8,128]{3,2,1,0:T(8,128)(2,1)} copy(bf16[1,192,8,128]{3,1,2,0:T(8,128)(2,1)S(1)} %bitcast.15) | data formatting | bytes 786432
  48.9 1.7 %widen.1 = (f32[192,1728]{1,0:T(8,128)}, f32[192,768]{1,0:T(8,128)}, f32[192,768]{1,0:T(8,128)}, f32[1,192]{1,0:T(1,128)}, f32[1,192]{1,0:T(1,128)}, /*index=5*/f32[1,768]{1,0:T(1,128)S(1)}) custom-call(bf16[2,2816,128]{2,1,0:T(8,128)(2,1)S(1)} %get-tuple-element.16.gathered), custom_call_target="tpu_custom_call" | custom-call | tf_op jit(solution)/shard_map/widen/pallas_call | solution.py:555
  50.6 0.6 %reduce = f32[768]{0:T(1024)} reduce(f32[1,768]{1,0:T(1,128)S(1)} %get-tuple-element.20, f32[]{:T(128)} %constant), dimensions={0}, to_apply=%get-tuple-element.20.reduce_sub_computation | reduce | bytes 6148 | tf_op jit(solution)/shard_map/widen/pallas_call | solution.py:555
Async XLA Ops:
  2.7 2.1 %copy-start = (bf16[192,1728]{1,0:T(8,128)(2,1)S(1)}, bf16[192,1728]{1,0:T(8,128)(2,1)}, u32[]{:S(2)}) copy-start(bf16[192,1728]{1,0:T(8,128)(2,1)} %cw.1) | copy-start | bytes 1990660
  2.7 2.1 %copy-start.1 = (bf16[768,192]{0,1:T(8,128)(2,1)S(1)}, bf16[768,192]{0,1:T(8,128)(2,1)}, u32[]{:S(2)}) copy-start(bf16[768,192]{0,1:T(8,128)(2,1)} %param.12) | copy-start | bytes 884740
  2.7 2.1 %copy-start.2 = (bf16[192,768]{1,0:T(8,128)(2,1)S(1)}, bf16[192,768]{1,0:T(8,128)(2,1)}, u32[]{:S(2)}) copy-start(bf16[192,768]{1,0:T(8,128)(2,1)} %pw.1) | copy-start | bytes 884740
  2.7 2.1 %copy-start.3 = (s32[2]{0:T(128)S(1)}, s32[2]{0:T(128)}, u32[]{:S(2)}) copy-start(s32[2]{0:T(128)} %key_ref.1) | copy-start | bytes 28

commit v5 on v4

--- a/solution.py
+++ b/solution.py
@@ -190,8 +190,9 @@
         firsts.append(push(source, buf1.at[f, pl.ds(0, half)], twin))
 
     def complete():
-        seconds = []
-        for f in ids:
+        seconds, thirds, fourths, fifths, final = [], [], [], [], []
+
+        def stage_1(f):
             half, part = halves[f], parts[f]
             firsts[f].wait_recv()
             kept = payload[at(flows[f][0] + core * half, half), :]
@@ -207,8 +208,7 @@
                 ]
             )
 
-        thirds = []
-        for f in ids:
+        def stage_2(f):
             part, own = parts[f], owns[f]
             total = s1[f, at(x * part, part), :].astype(F32)
             for d in range(1, n_x):
@@ -226,8 +226,7 @@
                 ]
             )
 
-        fourths = []
-        for f in ids:
+        def stage_3(f):
             part, own = parts[f], owns[f]
             total = s2[f, at(z * own, own), :].astype(F32)
             for d in range(1, n_z):
@@ -238,20 +237,25 @@
             mine[...] = total.astype(BF)
             fourths.append([push(mine, mine, z_peer(d)) for d in range(1, n_z)])
 
-        fifths = []
-        final = []
-        for f in ids:
+        def stage_4(f):
             for copy in fourths[f]:
                 copy.wait_recv()
             column = out.at[pipe, at(flows[f][0] + core * halves[f] + x * parts[f], parts[f])]
             fifths.append([push(column, column, xp_peer(*o)) for o in others])
             final.append(push(column, column, twin))
-        for f in ids:
+
+        def stage_5(f):
             for (dx, dp), copy in zip(others, fifths[f]):
                 copy.wait_recv()
                 start = flows[f][0] + core * halves[f] + ((x - dx + n_x) % n_x) * parts[f]
                 block = out.at[(pipe + dp) % 2, at(start, parts[f])]
                 final.append(push(block, block, twin))
+
+        stages = [stage_1, stage_2, stage_3, stage_4, stage_5]
+        for turn in range(len(flows) + len(stages) - 1):
+            for f in ids:
+                if 0 <= turn - f < len(stages):
+                    stages[turn - f](f)
         for copy in final:
             copy.wait_recv()
         for copy in started:

time: 51.4 us -> 59.6 us (1.16)
  Pallas kernels: 44.8 us -> 53 us
    pallas_call x1, Pallas kernels: 43.1 us -> 51.3 us  [per_device(): pl.pallas_call(functools.partial(compute_kernel, rows, cols, total_rows,...]
where the time goes in v5:
time: 59.6 us; the launch traced here: 59.4 us
  Pallas kernels  53 us (89%)
  local copies, waits for them, and re-layouts  5.1 us (9%)
  between operations  0.72 us (1%)
  other arithmetic  0.61 us (1%)
    pallas_call x1, Pallas kernels, per_device(): pl.pallas_call(functools.partial(compute_kernel, rows, cols, total_rows,...  51.3 us
    unnamed x11, local copies, waits for them, and re-layouts  4.11 us
    pallas_call x1, Pallas kernels, per_device(): pl.pallas_call(functools.partial(finish_kernel, taps, hidden), out_shape=...  1.66 us

profile of v5, /device:TPU:0, one launch (start us, length us, event | category | flops | bytes accessed | tf_op | source)
XLA Modules:
  0.0 59.4 jit_solution(15894049667548181525)
XLA Ops:
  0.6 0.8 %concatenate.3 = f32[1152]{0:T(1024)S(1)} concatenate(f32[192]{0:T(256)} %param.11, f32[768]{0:T(1024)} %param.13, f32[192]{0:T(256)} %param.15), dimensions={0} | concatenate | bytes 9216 | tf_op jit(solution)/shard_map/concatenate | solution.py:552
  1.4 1.0 %copy.26 = bf16[192,8,128]{2,0,1:T(8,128)(2,1)S(1)} copy(bf16[192,8,128]{2,1,0:T(8,128)(2,1)} %param.16) | data formatting | bytes 786432 | tf_op args[7]
  2.5 0.2 broadcast_in_dim.8.bias_ref
  2.7 0.0 copy-start
  2.7 0.0 copy-start.1
  2.7 0.0 copy-start.2
  2.7 0.0 copy-start.3
  2.7 2.0 %copy.25 = bf16[192,16,256]{2,0,1:T(8,128)(2,1)S(1)} copy(bf16[192,16,256]{2,1,0:T(8,128)(2,1)} %param.9) | data formatting | bytes 3145728 | tf_op args[0]
  4.8 0.0 copy-done
  4.8 0.0 copy-done.1
  4.8 0.0 copy-done.2
  4.8 0.0 copy-done.3
  4.8 51.3 %segment.1 = (bf16[8,192,128]{2,1,0:T(8,128)(2,1)S(1)}, bf16[2,2816,128]{2,1,0:T(8,128)(2,1)S(1)}) custom-call(s32[2]{0:T(128)S(1)} %copy-done.3, bf16[16,192,256]{2,1,0:T(8,128)(2,1)S(1)} %bitcast.13, bf16[192,1728]{1,0:T(8,128)(2,1)S(1)} %copy-done, bf16[192,768]{1,0:T(8,128)(2,1)S(1)} %bitcast.16, bf16[192,768]{1,0:T(8,128)(2,1)S(1)} %copy-done.2, ...), custom_call_target="tpu_custom_call" | custom-call | tf_op jit(solution)/shard_map/segment/pallas_call | solution.py:512
  56.1 1.0 %copy.22 = bf16[1,192,8,128]{3,2,1,0:T(8,128)(2,1)} copy(bf16[1,192,8,128]{3,1,2,0:T(8,128)(2,1)S(1)} %bitcast.15) | data formatting | bytes 786432
  57.1 1.7 %widen.1 = (f32[192,1728]{1,0:T(8,128)}, f32[192,768]{1,0:T(8,128)}, f32[192,768]{1,0:T(8,128)}, f32[1,192]{1,0:T(1,128)}, f32[1,192]{1,0:T(1,128)}, /*index=5*/f32[1,768]{1,0:T(1,128)S(1)}) custom-call(bf16[2,2816,128]{2,1,0:T(8,128)(2,1)S(1)} %get-tuple-element.16.gathered), custom_call_target="tpu_custom_call" | custom-call | tf_op jit(solution)/shard_map/widen/pallas_call | solution.py:559
  58.8 0.6 %reduce = f32[768]{0:T(1024)} reduce(f32[1,768]{1,0:T(1,128)S(1)} %get-tuple-element.20, f32[]{:T(128)} %constant), dimensions={0}, to_apply=%get-tuple-element.20.reduce_sub_computation | reduce | bytes 6148 | tf_op jit(solution)/shard_map/widen/pallas_call | solution.py:559
Async XLA Ops:
  2.7 2.1 %copy-start = (bf16[192,1728]{1,0:T(8,128)(2,1)S(1)}, bf16[192,1728]{1,0:T(8,128)(2,1)}, u32[]{:S(2)}) copy-start(bf16[192,1728]{1,0:T(8,128)(2,1)} %cw.1) | copy-start | bytes 1990660
  2.7 2.1 %copy-start.1 = (bf16[768,192]{0,1:T(8,128)(2,1)S(1)}, bf16[768,192]{0,1:T(8,128)(2,1)}, u32[]{:S(2)}) copy-start(bf16[768,192]{0,1:T(8,128)(2,1)} %param.12) | copy-start | bytes 884740
  2.7 2.1 %copy-start.2 = (bf16[192,768]{1,0:T(8,128)(2,1)S(1)}, bf16[192,768]{1,0:T(8,128)(2,1)}, u32[]{:S(2)}) copy-start(bf16[192,768]{1,0:T(8,128)(2,1)} %pw.1) | copy-start | bytes 884740
  2.7 2.1 %copy-start.3 = (s32[2]{0:T(128)S(1)}, s32[2]{0:T(128)}, u32[]{:S(2)}) copy-start(s32[2]{0:T(128)} %key_ref.1) | copy-start | bytes 28
